TPU v7x, 256 devices: a whole 4x4x8 slice. The times are simulated.
256 devices in a mesh: lon: 16 (over x_hi, y, core), lat: 16 (over x_lo, z).
Axes of the slice: x: 4 (x_hi: 2, x_lo: 2; x = x_hi * 2 + x_lo), y: 4, z: 8, core: 2. Of those that a mesh axis runs over, the one named last changes fastest.
Arguments:
- zonal_current: float32 [4096, 32768], P('lon', 'lat'), may hold values from -6 to 6
- meridional_current: float32 [4096, 32768], P('lon', 'lat'), may hold values from -6 to 6
- thermal_departure: float32 [4096, 32768], P('lon', 'lat'), may hold values from -6 to 6
- wet_point_flag: int32 [4096, 32768], P('lon', 'lat'), may hold values 0 or 1
Outputs:
- flux_east: float32 [4096, 32768], P('lon', 'lat')
- flux_north: float32 [4096, 32768], P('lon', 'lat')
All inputs are finite; a program needn't handle non-finite values. No bound on the sum of `wet_point_flag` on one device may be relied on, other than what follows from the above.
Results may differ from a plain program's by a relative error of at most 0.0003.
Values sent between devices are 32-bit elements; how exact they have to be, the bound alone decides.
No kernel may reach another device: no remote copies, remote signals or barrier semaphores. Data moves between devices by JAX's collectives and lax.ppermute only.
A program may use at most 192 MiB of HBM per device.

v0:
```python
import jax
import jax.numpy as jnp
from jax import lax
from jax.sharding import PartitionSpec as P

HALF = 64


def extended(x, sides, width, wrap):
    for axis, dim in sides:
        peers, length = (lax.axis_size(axis), x.shape[dim])
        up = [(i, (i + 1) % peers) for i in range(peers if wrap else peers - 1)]
        down = [(j, i) for i, j in up]
        last = lax.slice_in_dim(x, length - width, length, axis=dim)
        first = lax.slice_in_dim(x, 0, width, axis=dim)
        before = lax.ppermute(last, axis, up)
        after = lax.ppermute(first, axis, down)
        x = jnp.concatenate([before, x, after], axis=dim)
    return x


def band_matrix():
    block_len = 2 * HALF
    sigma = HALF / 2.0
    offsets = jnp.arange(2 * HALF + 1, dtype=jnp.float32) - HALF
    weight_sum = jnp.sum(jnp.exp(-offsets * offsets / (2.0 * sigma * sigma)))
    rows = jnp.arange(block_len, dtype=jnp.int32)[:, None]
    cols = jnp.arange(2 * block_len, dtype=jnp.int32)[None, :]
    dist = (cols - rows).astype(jnp.float32) - HALF
    inside = (cols - rows >= 0) & (cols - rows <= 2 * HALF)
    weights_band = jnp.where(
        inside, jnp.exp(-dist * dist / (2.0 * sigma * sigma)) / weight_sum, 0.0
    )
    taps_norm = jnp.exp(-offsets * offsets / (2.0 * sigma * sigma)) / weight_sum
    flux_scale = 1.0 / jnp.sum(taps_norm * taps_norm) ** 2
    return (weights_band, flux_scale)


def filter_last(padded, weights_band):
    block_len = 2 * HALF
    length = padded.shape[-1] - block_len
    lead = padded.shape[:-1]
    leading = padded[..., :length].reshape(lead + (length // block_len, block_len))
    trailing = padded[..., block_len:].reshape(lead + (length // block_len, block_len))
    result = jnp.einsum(
        "...bj,ij->...bi", leading, weights_band[:, :block_len], precision=lax.Precision.HIGHEST
    )
    result = result + jnp.einsum(
        "...bj,ij->...bi", trailing, weights_band[:, block_len:], precision=lax.Precision.HIGHEST
    )
    return result.reshape(lead + (length,))


def filter_lons(padded, weights_band):
    block_len = 2 * HALF
    nfields, total_rows, width = padded.shape
    length = total_rows - block_len
    leading = padded[:, :length].reshape(nfields, length // block_len, block_len, width)
    trailing = padded[:, block_len:].reshape(nfields, length // block_len, block_len, width)
    result = jnp.einsum(
        "ij,fbjr->fbir", weights_band[:, :block_len], leading, precision=lax.Precision.HIGHEST
    )
    result = result + jnp.einsum(
        "ij,fbjr->fbir", weights_band[:, block_len:], trailing, precision=lax.Precision.HIGHEST
    )
    return result.reshape(nfields, length, width)


def heat_fluxes(filtered, flux_scale):
    east = flux_scale * (filtered[3] - filtered[0] * filtered[2])
    north = flux_scale * (filtered[4] - filtered[1] * filtered[2])
    return jnp.stack([east, north])


def shards(zonal_current, meridional_current, thermal_departure, wet_point_flag):
    wet_cell_weights = wet_point_flag.astype(jnp.float32)
    ocean_only_zonal = wet_cell_weights * zonal_current
    ocean_only_meridional = wet_cell_weights * meridional_current
    ocean_only_heat = wet_cell_weights * thermal_departure
    weights_band, flux_scale = band_matrix()
    layered_quantities = jnp.stack(
        [
            ocean_only_zonal,
            ocean_only_meridional,
            ocean_only_heat,
            ocean_only_zonal * ocean_only_heat,
            ocean_only_meridional * ocean_only_heat,
        ]
    )
    padded = extended(layered_quantities, (("lon", 1),), HALF, True)
    zonal_done = filter_lons(padded, weights_band)
    rimmed = extended(zonal_done, (("lat", 2),), HALF, False)
    result = heat_fluxes(filter_last(rimmed, weights_band), flux_scale)
    return (result[0], result[1])


def solution(mesh):
    return jax.shard_map(
        shards,
        mesh=mesh,
        in_specs=(P("lon", "lat"), P("lon", "lat"), P("lon", "lat"), P("lon", "lat")),
        out_specs=(P("lon", "lat"), P("lon", "lat")),
        check_vma=False,
    )
```

profile of v0, /device:TPU:96, one launch (start us, length us, event | category | flops | bytes accessed | tf_op | source)
XLA Modules:
  0.0 162.2 jit_solution(2499623597200466696)
XLA Ops:
  0.7 2.7 %bitcast_dynamic-update-slice_fusion.4 = f32[5,256,2048]{2,1,0:T(8,128)S(1)} fusion(f32[256,2048]{1,0:T(8,128)} %param.4, s32[256,2048]{1,0:T(8,128)} %param.7), kind=kLoop, calls=%fused_computation.16 | loop fusion | flops 1048575 | bytes 6291456
  3.4 3.0 %bitcast_dynamic-update-slice_fusion.3 = f32[5,256,2048]{2,1,0:T(8,128)S(1)} fusion(f32[5,256,2048]{2,1,0:T(8,128)S(1)} %bitcast_dynamic-update-slice_fusion.4, f32[256,2048]{1,0:T(8,128)} %param.5, s32[256,2048]{1,0:T(8,128)} %param.7), kind=kLoop, calls=%fused_computation.15 | loop fusion | flops 1048576 | bytes 6291456
  6.7 0.7 bitcast_dynamic-update-slice_fusion.1
  7.4 0.7 bitcast_dynamic-update-slice_fusion
  8.0 0.6 fusion.18
  8.8 5.3 %collective-permute-start.1 = (f32[5,64,2048]{2,1,0:T(8,128)S(1)}, f32[5,64,2048]{2,1,0:T(8,128)S(1)}, u32[]{:S(2)}, u32[]{:S(2)}) collective-permute-start(f32[5,64,2048]{2,1,0:T(8,128)S(1)} %get-tuple-element.15), channel_id=1, source_target_pairs={{16,0},{32,16},{48,32},{64,48},{80,64},{96,80},{112,96},{128,112},... | collective-permute-start | bytes 7864328 | tf_op jit(solution)/shard_map/ppermute | solution.py:17
  14.7 0.7 fusion.7
  15.5 28.0 %collective-permute-done = f32[5,64,2048]{2,1,0:T(8,128)S(1)} collective-permute-done((f32[5,64,2048]{2,1,0:T(8,128)S(1)}, f32[5,64,2048]{2,1,0:T(8,128)S(1)}, u32[]{:S(2)}, u32[]{:S(2)}) %collective-permute-start) | collective-permute-done | bytes 2621472 | tf_op jit(solution)/shard_map/ppermute | solution.py:16
  43.5 7.0 %pad_maximum_fusion.3 = (f32[5,256,2048]{2,1,0:T(8,128)S(1)}, f32[5,256,2048]{2,1,0:T(8,128)S(1)}) fusion(f32[5,256,2048]{2,1,0:T(8,128)} %copy-done.1, f32[5,64,2048]{2,1,0:T(8,128)S(1)} %collective-permute-done, f32[5,64,2048]{2,1,0:T(8,128)S(1)} %collective-permute-done.1), kind=kLoop, calls=%fused_computation.3 | loop fusion | flops 5242880 | bytes 36700160 | tf_op jit(solution)/shard_map/concatenate | solution.py:18
  50.5 16.7 %fusion.12 = f32[5,2,2048,128]{2,3,1,0:T(8,128)} fusion(f32[5,2,128,2048]{3,2,1,0:T(8,128)S(1)} %bitcast.36, f32[128,256]{1,0:T(8,128)S(1)} %fusion.7), kind=kOutput, calls=%fused_computation.32 | convolution fusion | flops 4026531840 | bytes 21037056 | tf_op jit(solution)/shard_map/ij,fbjr->fbir/dot_general | solution.py:63
  67.2 15.1 %convolution_add_fusion = f32[5,2,2048,128]{2,3,1,0:T(8,128)} fusion(f32[5,2,2048,128]{2,3,1,0:T(8,128)} %fusion.12, f32[5,2,128,2048]{3,2,1,0:T(8,128)S(1)} %bitcast.37, f32[128,256]{1,0:T(8,128)S(1)} %fusion.7), kind=kOutput, calls=%fused_computation.4 | convolution fusion | flops 4029153280 | bytes 31522816 | tf_op jit(solution)/shard_map/ij,fbjr->fbir/dot_general | solution.py:60
  82.3 11.2 %copy.8 = f32[5,256,2048]{1,2,0:T(8,128)} copy(f32[5,256,2048]{2,1,0:T(8,128)} %bitcast.39) | data formatting | bytes 20971520 | tf_op jit(solution)/shard_map/reshape | solution.py:66
  93.5 1.1 fusion.17
  94.6 5.0 %collective-permute-start.2 = (f32[5,256,64]{1,2,0:T(8,128)S(1)}, f32[5,256,64]{1,2,0:T(8,128)S(1)}, u32[]{:S(2)}, u32[]{:S(2)}) collective-permute-start(f32[5,256,64]{1,2,0:T(8,128)S(1)} %get-tuple-element.10), channel_id=1, source_target_pairs={{0,1},{1,2},{2,3},{3,4},{4,5},{5,6},{6,7},{7,8},{8,9},{9,10},{10,1... | collective-permute-start | bytes 983048 | tf_op jit(solution)/shard_map/ppermute | solution.py:16
  99.7 2.1 %collective-permute-start.3 = (f32[5,256,64]{1,2,0:T(8,128)S(1)}, f32[5,256,64]{1,2,0:T(8,128)S(1)}, u32[]{:S(2)}, u32[]{:S(2)}) collective-permute-start(f32[5,256,64]{1,2,0:T(8,128)S(1)} %get-tuple-element.11), channel_id=1, source_target_pairs={{1,0},{2,1},{3,2},{4,3},{5,4},{6,5},{7,6},{8,7},{9,8},{10,9},{11,1... | collective-permute-start | bytes 983048 | tf_op jit(solution)/shard_map/ppermute | solution.py:17
  101.8 1.3 fusion.15
  104.4 0.7 collective-permute-done.2
  105.2 5.3 %collective-permute-done.3 = f32[5,256,64]{1,2,0:T(8,128)S(1)} collective-permute-done((f32[5,256,64]{1,2,0:T(8,128)S(1)}, f32[5,256,64]{1,2,0:T(8,128)S(1)}, u32[]{:S(2)}, u32[]{:S(2)}) %collective-permute-start.3) | collective-permute-done | bytes 327712 | tf_op jit(solution)/shard_map/ppermute | solution.py:17
  110.5 12.3 %pad_maximum_fusion.1 = (f32[5,256,2048]{1,2,0:T(8,128)S(1)}, f32[5,256,2048]{1,2,0:T(8,128)}) fusion(f32[5,256,2048]{1,2,0:T(8,128)} %copy.8, f32[5,256,64]{1,2,0:T(8,128)S(1)} %collective-permute-done.2, f32[5,256,64]{1,2,0:T(8,128)S(1)} %collective-permute-done.3), kind=kLoop, calls=%fused_computation.1 | loop fusion | flops 5242880 | bytes 32112640 | tf_op jit(solution)/shard_map/concatenate | solution.py:18
  122.8 14.7 %fusion.11 = f32[5,256,16,128]{1,3,2,0:T(8,128)} fusion(f32[5,256,16,128]{1,3,2,0:T(8,128)} %bitcast.38, f32[128,256]{1,0:T(8,128)S(1)} %fusion.7), kind=kOutput, calls=%fused_computation.31 | convolution fusion | flops 4026531840 | bytes 21037056 | tf_op jit(solution)/shard_map/...bj,ij->...bi/dot_general | solution.py:48
  137.5 13.6 %convolution_add_fusion.1 = f32[5,256,16,128]{1,3,2,0:T(8,128)} fusion(f32[5,256,16,128]{1,3,2,0:T(8,128)} %fusion.11, f32[5,256,16,128]{1,3,2,0:T(8,128)S(1)} %bitcast.35, f32[128,256]{1,0:T(8,128)S(1)} %fusion.7), kind=kOutput, calls=%fused_computation.5 | convolution fusion | flops 4029153280 | bytes 31522816 | tf_op jit(solution)/shard_map/...bj,ij->...bi/dot_general | solution.py:45
  151.1 6.4 %fusion.1 = (f32[1,256,16,128]{1,3,2,0:T(8,128)S(1)}, f32[1,256,16,128]{1,3,2,0:T(8,128)}) fusion(f32[5,256,16,128]{1,3,2,0:T(8,128)} %convolution_add_fusion.1, f32[]{:T(128)S(6)} %div.30), kind=kLoop, calls=%fused_computation.8 | loop fusion | flops 3145728 | bytes 14680068 | tf_op jit(solution)/shard_map/mul | solution.py:71
  157.5 2.9 %copy.14 = f32[256,2048]{1,0:T(8,128)} copy(f32[256,2048]{0,1:T(8,128)} %bitcast.41) | data formatting | bytes 4194304
  160.4 1.8 %copy.15 = f32[256,2048]{1,0:T(8,128)} copy(f32[256,2048]{0,1:T(8,128)S(1)} %bitcast.40) | data formatting | bytes 4194304
  (14 shorter events, 1.0 us)
Async XLA Ops:
  0.6 6.0 %copy-start.3 = (f32[256,2048]{1,0:T(8,128)S(1)}, f32[256,2048]{1,0:T(8,128)}, u32[]{:S(2)}) copy-start(f32[256,2048]{1,0:T(8,128)} %param.4) | copy-start | bytes 6291460
  0.6 5.7 %copy-start = (s32[256,2048]{1,0:T(8,128)S(1)}, s32[256,2048]{1,0:T(8,128)}, u32[]{:S(2)}) copy-start(s32[256,2048]{1,0:T(8,128)} %param.7) | copy-start | bytes 6291460
  0.7 5.7 %copy-start.2 = (f32[256,2048]{1,0:T(8,128)S(1)}, f32[256,2048]{1,0:T(8,128)}, u32[]{:S(2)}) copy-start(f32[256,2048]{1,0:T(8,128)} %param.6) | copy-start | bytes 6291460
  3.4 4.0 %copy-start.4 = (f32[256,2048]{1,0:T(8,128)S(1)}, f32[256,2048]{1,0:T(8,128)}, u32[]{:S(2)}) copy-start(f32[256,2048]{1,0:T(8,128)} %param.5) | copy-start | bytes 6291460
  8.0 35.4 %copy-start.1 = (f32[5,256,2048]{2,1,0:T(8,128)}, f32[5,256,2048]{2,1,0:T(8,128)S(1)}, u32[]{:S(2)}) copy-start(f32[5,256,2048]{2,1,0:T(8,128)S(1)} %bitcast_dynamic-update-slice_fusion) | copy-start | bytes 31457284
  8.7 34.8 %collective-permute-start = (f32[5,64,2048]{2,1,0:T(8,128)S(1)}, f32[5,64,2048]{2,1,0:T(8,128)S(1)}, u32[]{:S(2)}, u32[]{:S(2)}) collective-permute-start(f32[5,64,2048]{2,1,0:T(8,128)S(1)} %get-tuple-element.14), channel_id=1, source_target_pairs={{0,16},{16,32},{32,48},{48,64},{64,80},{80,96},{96,112},{112,128},... | collective-permute-start | bytes 7864328 | tf_op jit(solution)/shard_map/ppermute | solution.py:16
  8.8 34.7 %collective-permute-start.1 = (f32[5,64,2048]{2,1,0:T(8,128)S(1)}, f32[5,64,2048]{2,1,0:T(8,128)S(1)}, u32[]{:S(2)}, u32[]{:S(2)}) collective-permute-start(f32[5,64,2048]{2,1,0:T(8,128)S(1)} %get-tuple-element.15), channel_id=1, source_target_pairs={{16,0},{32,16},{48,32},{64,48},{80,64},{96,80},{112,96},{128,112},... | collective-permute-start | bytes 7864328 | tf_op jit(solution)/shard_map/ppermute | solution.py:17
  94.6 10.5 %collective-permute-start.2 = (f32[5,256,64]{1,2,0:T(8,128)S(1)}, f32[5,256,64]{1,2,0:T(8,128)S(1)}, u32[]{:S(2)}, u32[]{:S(2)}) collective-permute-start(f32[5,256,64]{1,2,0:T(8,128)S(1)} %get-tuple-element.10), channel_id=1, source_target_pairs={{0,1},{1,2},{2,3},{3,4},{4,5},{5,6},{6,7},{7,8},{8,9},{9,10},{10,1... | collective-permute-start | bytes 983048 | tf_op jit(solution)/shard_map/ppermute | solution.py:16
  99.7 10.8 %collective-permute-start.3 = (f32[5,256,64]{1,2,0:T(8,128)S(1)}, f32[5,256,64]{1,2,0:T(8,128)S(1)}, u32[]{:S(2)}, u32[]{:S(2)}) collective-permute-start(f32[5,256,64]{1,2,0:T(8,128)S(1)} %get-tuple-element.11), channel_id=1, source_target_pairs={{1,0},{2,1},{3,2},{4,3},{5,4},{6,5},{7,6},{8,7},{9,8},{10,9},{11,1... | collective-permute-start | bytes 983048 | tf_op jit(solution)/shard_map/ppermute | solution.py:17
where the time goes:
time: 164 us; the launch traced here: 162 us
  matrix products  60 us (37%)
  other arithmetic  35.6 us (22%)
  waiting for transfers between devices  34 us (21%)
  local copies, waits for them, and re-layouts  17.7 us (11%)
  starting transfers between devices  12.6 us (8%)
  between operations  2.13 us (1%)
    ppermute x2, waiting for transfers between devices, extended(): before = lax.ppermute(last, axis, up)  28.7 us
    concatenate x2, other arithmetic, extended(): x = jnp.concatenate([before, x, after], axis=dim)  19.4 us
    dot_general x1, matrix products, filter_lons(): jnp.einsum('ij,fbjr->fbir', weights_band[:, block_len:], trailing, precis...  16.7 us
    dot_general x1, matrix products, filter_lons(): jnp.einsum('ij,fbjr->fbir', weights_band[:, :block_len], leading, precisi...  15.1 us
    dot_general x1, matrix products, filter_last(): jnp.einsum('...bj,ij->...bi', trailing, weights_band[:, block_len:], prec...  14.7 us
    dot_general x1, matrix products, filter_last(): jnp.einsum('...bj,ij->...bi', leading, weights_band[:, :block_len], preci...  13.6 us
    reshape x1, local copies, waits for them, and re-layouts, filter_lons(): return result.reshape(nfields, length, width)  11.2 us
    ppermute x2, starting transfers between devices, extended(): after = lax.ppermute(first, axis, down)  7.49 us
  transfers between devices with their start and end apart: 4, of which 3 were waited for; matrix products, arithmetic and copies ran while one was open for 2% of the time, Pallas kernels for 0%

commit v1 on v0

v1 whole, which is shorter than its diff:
```python
import functools

import jax
import jax.numpy as jnp
import ml_dtypes
import numpy as np
from jax import lax
from jax.experimental import pallas as pl
from jax.experimental.pallas import tpu as pltpu
from jax.sharding import PartitionSpec as P

HALF = 64
BLK = 2 * HALF
ROWS = 256
COLS = 2048
NB = COLS // BLK
EXT = COLS + BLK
CW = 256
NJ = COLS // CW
MID = ROWS - BLK
SPLIT = 1280
BF = jnp.bfloat16
F32 = jnp.float32


def taps_np():
    k = np.arange(-HALF, HALF + 1, dtype=np.float64)
    sigma = HALF / 2.0
    g = np.exp(-k * k / (2.0 * sigma * sigma))
    return g / g.sum()


def toeplitz(rows, cols, shift):
    g = taps_np()
    k = np.arange(cols)[None, :] - np.arange(rows)[:, None] + shift
    return np.where(np.abs(k) <= HALF, g[np.clip(k + HALF, 0, 2 * HALF)], 0.0)


def hi_lo(a):
    a = a.astype(np.float32)
    hi = a.astype(ml_dtypes.bfloat16)
    lo = (a - hi.astype(np.float32)).astype(ml_dtypes.bfloat16)
    return hi, lo


SCALE = float(1.0 / np.sum(taps_np() ** 2) ** 2)


def split(x):
    hi = x.astype(BF)
    lo = (x - hi.astype(F32)).astype(BF)
    return hi, lo


def dot(a, b):
    return jnp.dot(a, b, preferred_element_type=F32)


def five(u, v, t):
    return (u, v, t, u * t, v * t)


def lat_window(zh, zl, w, start, rows):
    cols = pl.ds(start, 2 * BLK)
    r = dot(zh[:, cols], w) + dot(zl[:, cols], w)
    f = (r[:, :BLK] + r[:, BLK:]).reshape(5, rows, BLK)
    east = SCALE * (f[3] - f[0] * f[2])
    north = SCALE * (f[4] - f[1] * f[2])
    return pltpu.roll(east, HALF, 1), pltpu.roll(north, HALF, 1)


def first_half(shape):
    return lax.broadcasted_iota(jnp.int32, shape, 1) < HALF


def lat_pair(zh, zl, w, carry, fo, j, rows):
    low = first_half((rows, BLK))
    base = pl.multiple_of(j * CW, CW)
    pair0 = lat_window(zh, zl, w, base, rows)
    pair1 = lat_window(zh, zl, w, base + BLK, rows)
    for q in range(2):
        fo[q, :, pl.ds(base, BLK)] = jnp.where(low, carry[q], pair0[q])
        fo[q, :, pl.ds(base + BLK, BLK)] = jnp.where(low, pair0[q], pair1[q])
        carry[q] = pair1[q]


def lat_last(zh, zl, w, carry, fo, rows):
    low = first_half((rows, BLK))
    pair = lat_window(zh, zl, w, COLS, rows)
    for q in range(2):
        fo[q, :, pl.ds(COLS, BLK)] = jnp.where(low, carry[q], pair[q])


def interior_kernel(u, v, t, m, wrap, g, w_ref, e_out, n_out, zp_out,
                    ub, vb, tb, mb, zh, zl, zps, fo, carry, sem_in, sem_out, sem_e, sem_n):
    w = w_ref[...]

    def in_copies(j):
        cols = pl.ds(pl.multiple_of(j * CW, CW), CW)
        return [
            pltpu.make_async_copy(src.at[:, cols], dst.at[:, cols], sem_in.at[i, j])
            for i, (src, dst) in enumerate(((u, ub), (v, vb), (t, tb), (m, mb)))
        ]

    def zp_copy(j):
        cols = pl.ds(pl.multiple_of(j * CW, CW), CW)
        return pltpu.make_async_copy(zps.at[:, :, cols], zp_out.at[:, :, cols], sem_out.at[j])

    def out_copies(j):
        src = pl.ds(pl.multiple_of(j * CW, BLK), CW)
        dst = pl.ds(pl.multiple_of(j * CW - BLK, BLK), CW)
        rows = pl.ds(HALF, MID)
        return [
            pltpu.make_async_copy(fo.at[0, :, src], e_out.at[rows, dst], sem_e.at[j]),
            pltpu.make_async_copy(fo.at[1, :, src], n_out.at[rows, dst], sem_n.at[j]),
        ]

    def end_copies():
        rows = pl.ds(HALF, MID)
        done = []
        for q, (out, sem) in enumerate(((e_out, sem_e), (n_out, sem_n))):
            done.append(pltpu.make_async_copy(
                fo.at[q, :, pl.ds(BLK, BLK)], out.at[rows, pl.ds(0, BLK)], sem.at[0]))
            done.append(pltpu.make_async_copy(
                fo.at[q, :, pl.ds(COLS, BLK)], out.at[rows, pl.ds(COLS - BLK, BLK)], sem.at[NJ]))
        return done

    def zonal_fields(fields, stores, zcols, width):
        ghl = g[...]
        for f, x in enumerate(fields):
            hi, lo = split(x)
            r = dot(ghl, hi)
            z = r[:ROWS] + r[ROWS:] + dot(ghl[:ROWS], lo)
            zps[f, 0:HALF, zcols] = z[0:HALF]
            zps[f, HALF:BLK, zcols] = z[ROWS - HALF:]
            a, b = split(z[HALF:ROWS - HALF])
            for s in stores:
                zh[f * MID:(f + 1) * MID, s] = a
                zl[f * MID:(f + 1) * MID, s] = b

    def zonal(j):
        cols = pl.ds(pl.multiple_of(j * CW, CW), CW)
        wet = mb[:, cols].astype(F32)
        fields = five(wet * ub[:, cols], wet * vb[:, cols], wet * tb[:, cols])
        zonal_fields(fields, [pl.ds(pl.multiple_of(j * CW + BLK, BLK), CW)], cols, CW)

    for j in range(NJ):
        for copy in in_copies(j):
            copy.start()
    zonal_fields(five(wrap[0], wrap[1], wrap[2]), [pl.ds(0, BLK), pl.ds(COLS + BLK, BLK)], pl.ds(COLS, BLK), BLK)
    wrap_copy = pltpu.make_async_copy(
        zps.at[:, :, pl.ds(COLS, BLK)], zp_out.at[:, :, pl.ds(COLS, BLK)], sem_out.at[NJ])
    wrap_copy.start()

    def arrive(j):
        for copy in in_copies(j):
            copy.wait()

    arrive(0)
    zonal(0)
    zp_copy(0).start()

    def step(j, _):
        arrive(j)
        lat_pair(zh, zl, w, carry, fo, j - 1, MID)
        zonal(j)
        zp_copy(j).start()

        @pl.when(j > 1)
        def _():
            for copy in out_copies(j - 1):
                copy.start()

        return 0

    lax.fori_loop(1, NJ, step, 0)
    lat_pair(zh, zl, w, carry, fo, NJ - 1, MID)
    for copy in out_copies(NJ - 1):
        copy.start()
    lat_last(zh, zl, w, carry, fo, MID)
    for copy in end_copies():
        copy.start()
    wrap_copy.wait()
    for j in range(NJ):
        zp_copy(j).wait()
    for j in range(1, NJ):
        for copy in out_copies(j):
            copy.wait()
    for copy in end_copies():
        copy.wait()


def edge_kernel(npieces, *refs):
    sel_ref, e_in, n_in, zp = refs[:4]
    pieces = refs[4:4 + npieces]
    (gx, w_ref, e_out, n_out, hb, zpb, zh, zl, fo, carry,
     sem_h, sem_z, sem_e, sem_n) = refs[4 + npieces:]
    sel = sel_ref[0]
    w = w_ref[...]
    zrow = pl.multiple_of(sel * HALF, HALF)
    orow = pl.multiple_of(sel * (ROWS - HALF), HALF)
    starts = [0]
    for p in pieces:
        starts.append(starts[-1] + p.shape[2])
    chunks = [(COLS, BLK)] + [(j * CW, CW) for j in range(NJ)]

    def copies(i):
        start, width = chunks[i]
        for p, s in zip(pieces, starts):
            if s <= start and start + width <= s + p.shape[2]:
                return [
                    pltpu.make_async_copy(
                        p.at[:, :, pl.ds(start - s, width)], hb.at[:, :, pl.ds(start, width)], sem_h.at[i]),
                    pltpu.make_async_copy(
                        zp.at[:, pl.ds(zrow, HALF), pl.ds(start, width)],
                        zpb.at[:, :, pl.ds(start, width)], sem_z.at[i]),
                ]
        raise ValueError(start)

    for i in range(NJ + 1):
        for copy in copies(i):
            copy.start()
    gmat = gx[sel]

    def zonal_chunk(cols, stores):
        for f, x in enumerate(five(hb[0, :, cols], hb[1, :, cols], hb[2, :, cols])):
            hi, lo = split(x)
            z = zpb[f, :, cols] + dot(gmat, jnp.concatenate([hi, lo, hi], axis=0))
            a, b = split(z)
            for s in stores:
                zh[f * HALF:(f + 1) * HALF, s] = a
                zl[f * HALF:(f + 1) * HALF, s] = b

    def out_copies(j):
        src = pl.ds(j * CW, CW)
        dst = pl.ds(j * CW - BLK, CW)
        rows = pl.ds(orow, HALF)
        return [
            pltpu.make_async_copy(fo.at[0, :, src], e_out.at[rows, dst], sem_e.at[j]),
            pltpu.make_async_copy(fo.at[1, :, src], n_out.at[rows, dst], sem_n.at[j]),
        ]

    def end_copies():
        rows = pl.ds(orow, HALF)
        done = []
        for q, (out, sem) in enumerate(((e_out, sem_e), (n_out, sem_n))):
            done.append(pltpu.make_async_copy(
                fo.at[q, :, pl.ds(BLK, BLK)], out.at[rows, pl.ds(0, BLK)], sem.at[0]))
            done.append(pltpu.make_async_copy(
                fo.at[q, :, pl.ds(COLS, BLK)], out.at[rows, pl.ds(COLS - BLK, BLK)], sem.at[NJ]))
        return done

    for copy in copies(0):
        copy.wait()
    zonal_chunk(pl.ds(COLS, BLK), [pl.ds(0, BLK), pl.ds(COLS + BLK, BLK)])
    for j in range(NJ):
        for copy in copies(j + 1):
            copy.wait()
        zonal_chunk(pl.ds(j * CW, CW), [pl.ds(j * CW + BLK, CW)])
        lat_pair(zh, zl, w, carry, fo, j, HALF)
        if j > 0:
            for copy in out_copies(j):
                copy.start()
    lat_last(zh, zl, w, carry, fo, HALF)
    for copy in end_copies():
        copy.start()
    for j in range(1, NJ):
        for copy in out_copies(j):
            copy.wait()
    for copy in end_copies():
        copy.wait()


ANY = pl.BlockSpec(memory_space=pl.ANY)
VMEM = pl.BlockSpec(memory_space=pltpu.VMEM)
SMEM = pl.BlockSpec(memory_space=pltpu.SMEM)


def lat_matrix():
    hi, lo = hi_lo(toeplitz(BLK, 2 * BLK, -HALF).T)
    return jnp.asarray(np.concatenate([hi, lo], axis=1))


def interior(u, v, t, m, wrap):
    hi, lo = hi_lo(toeplitz(ROWS, ROWS, 0))
    g = jnp.asarray(np.concatenate([hi, lo], axis=0))
    flux = jax.ShapeDtypeStruct((ROWS, COLS), F32)
    return pl.pallas_call(
        interior_kernel,
        out_shape=(flux, flux, jax.ShapeDtypeStruct((5, BLK, EXT), F32)),
        in_specs=[ANY] * 4 + [VMEM] * 3,
        out_specs=(ANY, ANY, ANY),
        scratch_shapes=[
            pltpu.VMEM((ROWS, COLS), F32),
            pltpu.VMEM((ROWS, COLS), F32),
            pltpu.VMEM((ROWS, COLS), F32),
            pltpu.VMEM((ROWS, COLS), jnp.int32),
            pltpu.VMEM((5 * MID, EXT + BLK), BF),
            pltpu.VMEM((5 * MID, EXT + BLK), BF),
            pltpu.VMEM((5, BLK, EXT), F32),
            pltpu.VMEM((2, MID, EXT), F32),
            pltpu.VMEM((2, MID, BLK), F32),
            pltpu.SemaphoreType.DMA((4, NJ)),
            pltpu.SemaphoreType.DMA((NJ + 1,)),
            pltpu.SemaphoreType.DMA((NJ + 1,)),
            pltpu.SemaphoreType.DMA((NJ + 1,)),
        ],
        compiler_params=pltpu.CompilerParams(vmem_limit_bytes=40 * 2**20),
        cost_estimate=pl.CostEstimate(flops=7_000_000_000, bytes_accessed=16 * 2**20, transcendentals=0),
        name="interior",
    )(u, v, t, m, wrap, g, lat_matrix())


def edge(sel, east, north, zp, pieces, name):
    mats = []
    for shift in (-HALF, HALF):
        hi, lo = hi_lo(toeplitz(HALF, HALF, shift))
        mats.append(np.concatenate([hi, hi, lo], axis=1))
    gx = jnp.asarray(np.stack(mats))
    flux = jax.ShapeDtypeStruct((ROWS, COLS), F32)
    return pl.pallas_call(
        functools.partial(edge_kernel, len(pieces)),
        out_shape=(flux, flux),
        in_specs=[SMEM] + [ANY] * (3 + len(pieces)) + [VMEM] * 2,
        out_specs=(ANY, ANY),
        scratch_shapes=[
            pltpu.VMEM((3, HALF, EXT), F32),
            pltpu.VMEM((5, HALF, EXT), F32),
            pltpu.VMEM((5 * HALF, EXT + BLK), BF),
            pltpu.VMEM((5 * HALF, EXT + BLK), BF),
            pltpu.VMEM((2, HALF, EXT), F32),
            pltpu.VMEM((2, HALF, BLK), F32),
            pltpu.SemaphoreType.DMA((NJ + 1,)),
            pltpu.SemaphoreType.DMA((NJ + 1,)),
            pltpu.SemaphoreType.DMA((NJ + 1,)),
            pltpu.SemaphoreType.DMA((NJ + 1,)),
        ],
        input_output_aliases={1: 0, 2: 1},
        compiler_params=pltpu.CompilerParams(vmem_limit_bytes=40 * 2**20),
        cost_estimate=pl.CostEstimate(flops=2_000_000_000, bytes_accessed=5 * 2**20, transcendentals=0),
        name=name,
    )(sel, east, north, zp, *pieces, gx, lat_matrix())


def shards(u, v, t, m):
    nlon, nlat = lax.axis_size("lon"), lax.axis_size("lat")
    core = lax.axis_index("lon") % 2
    xoff = core * (ROWS - HALF)
    ioff = (1 - core) * (ROWS - HALF)
    across = [(i, (i + 1) % nlon if i % 2 else (i - 1) % nlon) for i in range(nlon)]
    inside = [(i, i + 1 - 2 * (i % 2)) for i in range(nlon)]
    up = [(i, i + 1) for i in range(nlat - 1)]
    down = [(j, i) for i, j in up]

    def masked(row, nrows, lo, hi):
        def cut(a):
            return lax.dynamic_slice(a, (row, lo), (nrows, hi - lo))

        wet = cut(m).astype(F32)
        return jnp.stack([wet * cut(u), wet * cut(v), wet * cut(t)])

    x1 = lax.ppermute(masked(xoff, HALF, 0, SPLIT), "lon", across)
    from_left = lax.ppermute(masked(0, ROWS, COLS - BLK, COLS), "lat", up)
    from_right = lax.ppermute(masked(0, ROWS, 0, BLK), "lat", down)
    lane = lax.broadcasted_iota(jnp.int32, (3, ROWS, BLK), 2)
    wrap = jnp.where(lane < HALF, from_right, from_left)

    def corner(row):
        return lax.dynamic_slice(wrap, (0, row, 0), (3, HALF, BLK))

    x2 = jnp.concatenate([masked(xoff, HALF, SPLIT, COLS), corner(xoff)], axis=2)
    x2 = lax.ppermute(x2, "lon", across)
    near = jnp.concatenate([masked(ioff, HALF, 0, COLS), corner(ioff)], axis=2)
    near = lax.ppermute(near, "lon", inside)
    east, north, zp = interior(u, v, t, m, wrap)
    sel = core.astype(jnp.int32).reshape(1)
    east, north = edge(1 - sel, east, north, zp, (near,), "edge_near")
    return edge(sel, east, north, zp, (x1, x2), "edge_far")


def solution(mesh):
    return jax.shard_map(
        shards,
        mesh=mesh,
        in_specs=(P("lon", "lat"),) * 4,
        out_specs=(P("lon", "lat"),) * 2,
        check_vma=False,
    )
```

time: 164 us -> 57.3 us (0.35)
  matrix products: 60 us -> 0 us
  other arithmetic: 35.6 us -> 4.84 us
  Pallas kernels: 0 us -> 24.2 us
  waiting for transfers between devices: 34 us -> 10.1 us
  local copies, waits for them, and re-layouts: 17.7 us -> 4.07 us
    dot_general x4 -> x0, matrix products: 60 us -> none  [the longest x1 16.7 us: filter_lons(): jnp.einsum('ij,fbjr->fbir', weights_band[:, block_len:], trailing, precis...]
    pallas_call x0 -> x3, Pallas kernels: none -> 24.2 us  [the longest x1 12.3 us: interior(): pl.pallas_call(interior_kernel, out_shape=(flux, flux, jax.ShapeDtypeStru...]
    ppermute x4 -> x5, waiting for transfers between devices: 34 us -> 10.1 us  [the longest x1 5.47 us: shards(): from_right = lax.ppermute(masked(0, ROWS, 0, BLK), 'lat', down)]
    concatenate x2, other arithmetic: 19.4 us -> 0.17 us  [the longest x1 0.13 us: shards(): near = jnp.concatenate([masked(ioff, HALF, 0, COLS), corner(ioff)], axis=2)]
    reshape x1 -> x0, local copies, waits for them, and re-layouts: 11.2 us -> none  [filter_lons(): return result.reshape(nfields, length, width)]
    unnamed x4 -> x0, other arithmetic: 6.63 us -> none
    mul x1 -> x0, other arithmetic: 6.4 us -> none  [heat_fluxes(): north = flux_scale * (filtered[4] - filtered[1] * filtered[2])]
    another operation x1 -> x7, other arithmetic: 0.67 us -> 3.48 us  [masked(): return jnp.stack([wet * cut(u), wet * cut(v), wet * cut(t)])]
  transfers between devices with their start and end apart: 4 -> 5, of which waited for: 3 -> 2; matrix products, arithmetic and copies ran while one was open for 2% -> 3% of each run, Pallas kernels for 0% -> 32%
where the time goes in v1:
time: 57.3 us; the launch traced here: 57.1 us
  Pallas kernels  24.2 us (42%)
  starting transfers between devices  12.8 us (22%)
  waiting for transfers between devices  10.1 us (18%)
  other arithmetic  4.84 us (8%)
  local copies, waits for them, and re-layouts  4.07 us (7%)
  between operations  1.04 us (2%)
    pallas_call x1, Pallas kernels, interior(): pl.pallas_call(interior_kernel, out_shape=(flux, flux, jax.ShapeDtypeStru...  12.3 us
    pallas_call x2, Pallas kernels, edge(): pl.pallas_call(functools.partial(edge_kernel, len(pieces)), out_shape=(fl...  12 us
    ppermute x1, waiting for transfers between devices, shards(): from_right = lax.ppermute(masked(0, ROWS, 0, BLK), 'lat', down)  5.47 us
    ppermute x1, starting transfers between devices, shards(): from_left = lax.ppermute(masked(0, ROWS, COLS - BLK, COLS), 'lat', up)  5.04 us
    ppermute x1, waiting for transfers between devices, shards(): from_left = lax.ppermute(masked(0, ROWS, COLS - BLK, COLS), 'lat', up)  4.62 us
    ppermute x1, starting transfers between devices, shards(): x1 = lax.ppermute(masked(xoff, HALF, 0, SPLIT), 'lon', across)  4.23 us
    unnamed x16, local copies, waits for them, and re-layouts  4.04 us
    another operation x7, other arithmetic, masked(): return jnp.stack([wet * cut(u), wet * cut(v), wet * cut(t)])  3.48 us
  transfers between devices with their start and end apart: 5, of which 2 were waited for; matrix products, arithmetic and copies ran while one was open for 3% of the time, Pallas kernels for 32%

profile of v1, /device:TPU:96, one launch (start us, length us, event | category | flops | bytes accessed | tf_op | source)
XLA Modules:
  0.0 57.1 jit_solution(391153475294642581)
XLA Ops:
  0.6 1.5 %multiply_bitcast_fusion.11 = (f32[1,256,128]{2,1,0:T(8,128)S(1)}, f32[1,256,128]{2,1,0:T(8,128)S(1)}, f32[1,256,128]{2,1,0:T(8,128)S(1)}, f32[1,256,128]{2,1,0:...) fusion(f32[256,2048]{1,0:T(8,128)} %u.1, s32[256,2048]{1,0:T(8,128)} %m.1, f32[256,2048]{1,0:T(8,128)} %t.1, ...), kind=kLoop, calls=%fused_computation.17 | loop fusion | flops 262144 | bytes 1835008 | tf_op jit(solution)/shard_map/stack | solution.py:360
  2.2 5.0 %collective-permute-start.1 = (f32[3,256,128]{2,1,0:T(8,128)S(1)}, f32[3,256,128]{2,1,0:T(8,128)S(1)}, u32[]{:S(2)}, u32[]{:S(2)}) collective-permute-start(f32[3,256,128]{2,1,0:T(8,128)S(1)} %pad_maximum_fusion.4), channel_id=1, source_target_pairs={{0,1},{1,2},{2,3},{3,4},{4,5},{5,6},{6,7},{7,8},{8,9},{9,10},{10,1... | collective-permute-start | bytes 1179656 | tf_op jit(solution)/shard_map/ppermute | solution.py:363
  7.3 1.9 %collective-permute-start = (f32[3,256,128]{2,1,0:T(8,128)S(1)}, f32[3,256,128]{2,1,0:T(8,128)}, u32[]{:S(2)}, u32[]{:S(2)}) collective-permute-start(f32[3,256,128]{2,1,0:T(8,128)S(1)} %pad_maximum_fusion.3), channel_id=1, source_target_pairs={{1,0},{2,1},{3,2},{4,3},{5,4},{6,5},{7,6},{8,7},{9,8},{10,9},{11,1... | collective-permute-start | bytes 1179656 | tf_op jit(solution)/shard_map/ppermute | solution.py:364
  9.2 0.0 copy-start.4
  9.2 1.7 %multiply_bitcast_fusion.2 = (f32[1,64,2048]{2,1,0:T(8,128)S(1)}, f32[1,64,2048]{2,1,0:T(8,128)S(1)}, f32[1,64,2048]{2,1,0:T(8,128)S(1)}) fusion(f32[256,2048]{1,0:T(8,128)S(1)} %copy-done.1, s32[]{:T(128)S(6)} %select_n.17, s32[256,2048]{1,0:T(8,128)} %m.1, f32[256,2048]{1,0:T(8,128)} %t.1, f32[256,2048]{1,0:T(8,128)} %v.1), kind=kLoop, calls=%fused_computation.5 | loop fusion | flops 524288 | bytes 3670020 | tf_op jit(solution)/shard_map/stack | solution.py:360
  11.0 4.6 %collective-permute-done.1 = f32[3,256,128]{2,1,0:T(8,128)S(1)} collective-permute-done((f32[3,256,128]{2,1,0:T(8,128)S(1)}, f32[3,256,128]{2,1,0:T(8,128)S(1)}, u32[]{:S(2)}, u32[]{:S(2)}) %collective-permute-start.1) | collective-permute-done | bytes 393248 | tf_op jit(solution)/shard_map/ppermute | solution.py:363
  15.6 5.5 %collective-permute-done = f32[3,256,128]{2,1,0:T(8,128)} collective-permute-done((f32[3,256,128]{2,1,0:T(8,128)S(1)}, f32[3,256,128]{2,1,0:T(8,128)}, u32[]{:S(2)}, u32[]{:S(2)}) %collective-permute-start) | collective-permute-done | bytes 393248 | tf_op jit(solution)/shard_map/ppermute | solution.py:364
  21.0 1.2 %broadcast_select_fusion.wrap = f32[3,256,128]{2,1,0:T(8,128)S(1)} fusion(f32[3,256,128]{2,1,0:T(8,128)} %collective-permute-done, f32[3,256,128]{2,1,0:T(8,128)S(1)} %collective-permute-done.1, pred[128]{0:T(512)(128)(4,1)S(1)} %iota_compare_fusion), kind=kLoop, calls=%fused_computation.14 | loop fusion | flops 98304 | bytes 1179776 | tf_op jit(solution)/shard_map/jit(_where)/select_n | solution.py:366
  22.3 0.1 pad_maximum_fusion
  22.4 0.1 collective-permute-start.2
  22.5 0.2 copy-done.3
  22.8 1.2 %copy-done.2 = f32[256,2048]{1,0:T(8,128)S(1)} copy-done((f32[256,2048]{1,0:T(8,128)S(1)}, f32[256,2048]{1,0:T(8,128)}, u32[]{:S(2)}) %copy-start.2) | copy-done | bytes 2097176
  24.0 0.1 multiply_bitcast_fusion.5
  24.1 0.0 copy-start.5
  24.1 0.0 copy-start.7
  24.1 0.1 pad_maximum_fusion.1
  24.2 4.2 %collective-permute-start.3 = (f32[3,64,1280]{2,1,0:T(8,128)S(1)}, f32[3,64,1280]{2,1,0:T(8,128)S(1)}, u32[]{:S(2)}, u32[]{:S(2)}) collective-permute-start(f32[3,64,1280]{2,1,0:T(8,128)S(1)} %pad_maximum_fusion.1), channel_id=1, source_target_pairs={{0,240},{16,32},{32,16},{48,64},{64,48},{80,96},{96,80},{112,128},... | collective-permute-start | bytes 2949128 | tf_op jit(solution)/shard_map/ppermute | solution.py:362
  28.4 0.1 multiply_bitcast_fusion.8
  28.5 0.0 copy-start.6
  28.5 1.5 %collective-permute-start.4 = (f32[3,64,896]{2,1,0:T(8,128)S(1)}, f32[3,64,896]{2,1,0:T(8,128)S(1)}, u32[]{:S(2)}, u32[]{:S(2)}) collective-permute-start(f32[3,64,896]{2,1,0:T(8,128)S(1)} %pad_maximum_fusion.2), channel_id=1, source_target_pairs={{0,240},{16,32},{32,16},{48,64},{64,48},{80,96},{96,80},{112,128},... | collective-permute-start | bytes 2064392 | tf_op jit(solution)/shard_map/ppermute | solution.py:372
  30.0 12.3 %interior.1 = (f32[256,2048]{1,0:T(8,128)}, f32[256,2048]{1,0:T(8,128)}, f32[5,128,2176]{2,1,0:T(8,128)}) custom-call(f32[256,2048]{1,0:T(8,128)S(1)} %copy-done.1, f32[256,2048]{1,0:T(8,128)S(1)} %copy-done.2, f32[256,2048]{1,0:T(8,128)S(1)} %copy-done.3, s32[256,2048]{1,0:T(8,128)S(1)} %copy-done.4, f32[3,256,128]{2,1,0:T(8,128)S(1)} %broadcast_select_fusion.wrap, ...), custom_call_target="tpu_custom_call" | custom-call | flops 7000000000 | bytes 16777216 | tf_op jit(solution)/shard_map/interior/pallas_call | solution.py:288
  42.3 2.6 %copy-done = f32[5,128,2176]{2,1,0:T(8,128)S(1)} copy-done((f32[5,128,2176]{2,1,0:T(8,128)S(1)}, f32[5,128,2176]{2,1,0:T(8,128)}, u32[]{:S(2)}) %copy-start) | copy-done | bytes 5570584
  44.9 6.0 %edge_near.1 = (f32[256,2048]{1,0:T(8,128)}, f32[256,2048]{1,0:T(8,128)}) custom-call(s32[1]{0:T(128)S(6)} %sub.6.refs_0_, f32[256,2048]{1,0:T(8,128)} %get-tuple-element.7.refs_1_, f32[256,2048]{1,0:T(8,128)} %get-tuple-element.8.refs_2_, f32[5,128,2176]{2,1,0:T(8,128)S(1)} %copy-done, ...), custom_call_target="tpu_custom_call", output_to_operand_aliasing={{0}: (1, {}), {1}: (2, {})} | custom-call | flops 2000000000 | bytes 5242880 | tf_op jit(solution)/shard_map/edge_near/pallas_call | solution.py:321
  50.9 6.0 %edge_far.1 = (f32[256,2048]{1,0:T(8,128)}, f32[256,2048]{1,0:T(8,128)}) custom-call(s32[1]{0:T(128)} %bitcast.refs_0_, f32[256,2048]{1,0:T(8,128)} %get-tuple-element.10.refs_1_, f32[256,2048]{1,0:T(8,128)} %get-tuple-element.11.refs_2_, f32[5,128,2176]{2,1,0:T(8,128)S(1)} %copy-done, ...), custom_call_target="tpu_custom_call", output_to_operand_aliasing={{0}: (1, {}), {1}: (2, {})} | custom-call | flops 2000000000 | bytes 5242880 | tf_op jit(solution)/shard_map/edge_far/pallas_call | solution.py:321
  (17 shorter events, 0.2 us)
Async XLA Ops:
  0.6 8.6 %copy-start.1 = (f32[256,2048]{1,0:T(8,128)S(1)}, f32[256,2048]{1,0:T(8,128)}, u32[]{:S(2)}) copy-start(f32[256,2048]{1,0:T(8,128)} %u.1) | copy-start | bytes 6291460
  2.2 13.4 %collective-permute-start.1 = (f32[3,256,128]{2,1,0:T(8,128)S(1)}, f32[3,256,128]{2,1,0:T(8,128)S(1)}, u32[]{:S(2)}, u32[]{:S(2)}) collective-permute-start(f32[3,256,128]{2,1,0:T(8,128)S(1)} %pad_maximum_fusion.4), channel_id=1, source_target_pairs={{0,1},{1,2},{2,3},{3,4},{4,5},{5,6},{6,7},{7,8},{8,9},{9,10},{10,1... | collective-permute-start | bytes 1179656 | tf_op jit(solution)/shard_map/ppermute | solution.py:363
  7.3 13.8 %collective-permute-start = (f32[3,256,128]{2,1,0:T(8,128)S(1)}, f32[3,256,128]{2,1,0:T(8,128)}, u32[]{:S(2)}, u32[]{:S(2)}) collective-permute-start(f32[3,256,128]{2,1,0:T(8,128)S(1)} %pad_maximum_fusion.3), channel_id=1, source_target_pairs={{1,0},{2,1},{3,2},{4,3},{5,4},{6,5},{7,6},{8,7},{9,8},{10,9},{11,1... | collective-permute-start | bytes 1179656 | tf_op jit(solution)/shard_map/ppermute | solution.py:364
  9.2 13.3 %copy-start.4 = (s32[256,2048]{1,0:T(8,128)S(1)}, s32[256,2048]{1,0:T(8,128)}, u32[]{:S(2)}) copy-start(s32[256,2048]{1,0:T(8,128)} %m.1) | copy-start | bytes 6291460
  21.0 1.7 %copy-start.3 = (f32[256,2048]{1,0:T(8,128)S(1)}, f32[256,2048]{1,0:T(8,128)}, u32[]{:S(2)}) copy-start(f32[256,2048]{1,0:T(8,128)} %t.1) | copy-start | bytes 6291460
  22.2 1.7 %copy-start.2 = (f32[256,2048]{1,0:T(8,128)S(1)}, f32[256,2048]{1,0:T(8,128)}, u32[]{:S(2)}) copy-start(f32[256,2048]{1,0:T(8,128)} %v.1) | copy-start | bytes 6291460
  22.4 19.9 %collective-permute-start.2 = (f32[3,64,2176]{2,1,0:T(8,128)S(1)}, f32[3,64,2176]{2,1,0:T(8,128)S(1)}, u32[]{:S(2)}, u32[]{:S(2)}) collective-permute-start(f32[3,64,2176]{2,1,0:T(8,128)S(1)} %pad_maximum_fusion), channel_id=1, source_target_pairs={{0,16},{16,0},{32,48},{48,32},{64,80},{80,64},{96,112},{112,96},{1... | collective-permute-start | bytes 5013512 | tf_op jit(solution)/shard_map/ppermute | solution.py:374
  24.1 5.9 %copy-start.5 = (bf16[256,256]{1,0:T(8,128)(2,1)S(1)}, bf16[256,256]{1,0:T(8,128)(2,1)}, u32[]{:S(2)}) copy-start(bf16[256,256]{1,0:T(8,128)(2,1)} %constant.37.clone.w_ref.refs_6_.refs_7_) | copy-start | bytes 393220
  24.1 5.9 %copy-start.7 = (bf16[512,256]{1,0:T(8,128)(2,1)S(1)}, bf16[512,256]{1,0:T(8,128)(2,1)}, u32[]{:S(2)}) copy-start(bf16[512,256]{1,0:T(8,128)(2,1)} %constant.36.clone.g) | copy-start | bytes 786436
  24.2 26.7 %collective-permute-start.3 = (f32[3,64,1280]{2,1,0:T(8,128)S(1)}, f32[3,64,1280]{2,1,0:T(8,128)S(1)}, u32[]{:S(2)}, u32[]{:S(2)}) collective-permute-start(f32[3,64,1280]{2,1,0:T(8,128)S(1)} %pad_maximum_fusion.1), channel_id=1, source_target_pairs={{0,240},{16,32},{32,16},{48,64},{64,48},{80,96},{96,80},{112,128},... | collective-permute-start | bytes 2949128 | tf_op jit(solution)/shard_map/ppermute | solution.py:362
  28.5 13.8 %copy-start.6 = (bf16[2,64,192]{2,1,0:T(8,128)(2,1)S(1)}, bf16[2,64,192]{2,1,0:T(8,128)(2,1)}, u32[]{:S(2)}) copy-start(bf16[2,64,192]{2,1,0:T(8,128)(2,1)} %constant.38.clone.refs_5_.refs_6_) | copy-start | bytes 147460
  28.5 22.4 %collective-permute-start.4 = (f32[3,64,896]{2,1,0:T(8,128)S(1)}, f32[3,64,896]{2,1,0:T(8,128)S(1)}, u32[]{:S(2)}, u32[]{:S(2)}) collective-permute-start(f32[3,64,896]{2,1,0:T(8,128)S(1)} %pad_maximum_fusion.2), channel_id=1, source_target_pairs={{0,240},{16,32},{32,16},{48,64},{64,48},{80,96},{96,80},{112,128},... | collective-permute-start | bytes 2064392 | tf_op jit(solution)/shard_map/ppermute | solution.py:372
  42.3 2.6 %copy-start = (f32[5,128,2176]{2,1,0:T(8,128)S(1)}, f32[5,128,2176]{2,1,0:T(8,128)}, u32[]{:S(2)}) copy-start(f32[5,128,2176]{2,1,0:T(8,128)} %get-tuple-element.9.refs_3_) | copy-start | bytes 16711684

commit v2 on v0

v2 whole, which is shorter than its diff:
```python
import functools

import jax
import jax.numpy as jnp
import ml_dtypes
import numpy as np
from jax import lax
from jax.experimental import pallas as pl
from jax.experimental.pallas import tpu as pltpu
from jax.sharding import PartitionSpec as P

HALF = 64
BLK = 2 * HALF
ROWS = 256
COLS = 2048
NB = COLS // BLK
EXT = COLS + BLK
CW = 256
MID = ROWS - BLK
EW = 512
DW = 512
NEAR = (0, 768, 1536, COLS)
PREP_MIB = 8
MID_MIB = 6
EDGE_MIB = 8
ZONAL_MIB = 16
UNROLL_B = 7
BF = jnp.bfloat16
F32 = jnp.float32


def taps_np():
    k = np.arange(-HALF, HALF + 1, dtype=np.float64)
    sigma = HALF / 2.0
    g = np.exp(-k * k / (2.0 * sigma * sigma))
    return g / g.sum()


def toeplitz(rows, cols, shift):
    g = taps_np()
    k = np.arange(cols)[None, :] - np.arange(rows)[:, None] + shift
    return np.where(np.abs(k) <= HALF, g[np.clip(k + HALF, 0, 2 * HALF)], 0.0)


def hi_lo(a):
    a = a.astype(np.float32)
    hi = a.astype(ml_dtypes.bfloat16)
    lo = (a - hi.astype(np.float32)).astype(ml_dtypes.bfloat16)
    return hi, lo


SCALE = float(1.0 / np.sum(taps_np() ** 2) ** 2)


def split(x):
    hi = x.astype(BF)
    lo = (x - hi.astype(F32)).astype(BF)
    return hi, lo


def dot(a, b):
    return jnp.dot(a, b, preferred_element_type=F32)


def five(u, v, t):
    return (u, v, t, u * t, v * t)


def fluxes(zh, zl, w, rows):
    r = dot(zh, w) + dot(zl, w)
    f = (r[:, :BLK] + r[:, BLK:]).reshape(5, rows, BLK)
    east = SCALE * (f[3] - f[0] * f[2])
    north = SCALE * (f[4] - f[1] * f[2])
    return pltpu.roll(east, HALF, 1), pltpu.roll(north, HALF, 1)


def merge(fo, start, left, right, rows):
    low = lax.broadcasted_iota(jnp.int32, (rows, BLK), 1) < HALF
    for q in range(2):
        fo[q, :, pl.ds(start, BLK)] = jnp.where(low, left[q], right[q])


def zonal_local(g, fields, store):
    for f, x in enumerate(fields):
        hi, lo = split(x)
        r = dot(g, hi)
        store(f, r[:ROWS] + r[ROWS:] + dot(g[:ROWS], lo))


def prep_kernel(core, u, v, t, m, x1, to_right, to_left, rows, wet_rows, cols, wet_cols, sem):
    top = pl.ds(pl.multiple_of(core[0] * (ROWS - HALF), HALF), HALF)
    sides = (pl.ds(COLS - BLK, BLK), pl.ds(0, BLK))
    copies = [pltpu.make_async_copy(m.at[top, :], wet_rows, sem.at[0, 3])]
    copies += [pltpu.make_async_copy(a.at[top, :], rows.at[i], sem.at[0, i]) for i, a in enumerate((u, v, t))]
    for s, side in enumerate(sides):
        copies.append(pltpu.make_async_copy(m.at[:, side], wet_cols.at[s], sem.at[1 + s, 3]))
        copies += [pltpu.make_async_copy(a.at[:, side], cols.at[s, i], sem.at[1 + s, i])
                   for i, a in enumerate((u, v, t))]
    for copy in copies:
        copy.start()
    for copy in copies[:4]:
        copy.wait()
    wet = wet_rows[...].astype(F32)
    for i in range(3):
        x1[i] = wet * rows[i]
    for s, out in enumerate((to_right, to_left)):
        for copy in copies[4 + 4 * s:8 + 4 * s]:
            copy.wait()
        wet = wet_cols[s].astype(F32)
        for i in range(3):
            out[i] = wet * cols[s, i]


def zonal_kernel(core, u, v, t, m, g_ref, zh, zl, zp, *refs):
    *near, ub, vb, tb, mb, sem = refs
    g = g_ref[...]
    lower = core[0] == 0

    def copies(j):
        cols = pl.ds(j * DW, DW)
        return [
            pltpu.make_async_copy(src.at[:, cols], dst.at[:, cols], sem.at[i, j])
            for i, (src, dst) in enumerate(((u, ub), (v, vb), (t, tb), (m, mb)))
        ]

    for j in range(2):
        for copy in copies(j):
            copy.start()
    for j in range(COLS // CW):
        if j * CW % DW == 0:
            k = j * CW // DW
            for copy in copies(k):
                copy.wait()
            if k + 2 < COLS // DW:
                for copy in copies(k + 2):
                    copy.start()
        cols = pl.ds(j * CW, CW)
        wet = mb[:, cols].astype(F32)
        three = (wet * ub[:, cols], wet * vb[:, cols], wet * tb[:, cols])
        part = max(p for p, start in enumerate(NEAR) if start <= j * CW)
        for i, x in enumerate(three):
            near[part][i, :, pl.ds(j * CW - NEAR[part], CW)] = jnp.where(lower, x[ROWS - HALF:], x[:HALF])

        def store(f, z):
            zp[f, 0:HALF, cols] = z[0:HALF]
            zp[f, HALF:BLK, cols] = z[ROWS - HALF:]
            a, b = split(z[HALF:ROWS - HALF])
            zh[f * MID:(f + 1) * MID, cols] = a
            zl[f * MID:(f + 1) * MID, cols] = b

        zonal_local(g, five(*three), store)


def flux_copies(fo, e_out, n_out, row, rows, start, width, sem):
    cols = pl.ds(start, width)
    return [
        pltpu.make_async_copy(fo.at[q, :, cols], out.at[pl.ds(row, rows), cols], sem.at[q])
        for q, out in enumerate((e_out, n_out))
    ]


def middle_kernel(zh, zl, from_left, from_right, g_ref, w_ref, e_out, n_out, zpw,
                  zwh, zwl, fo, carry, sem):
    w = w_ref[...]
    low = lax.broadcasted_iota(jnp.int32, (ROWS, BLK), 1) < HALF

    def store(f, z):
        zpw[f, 0:HALF] = z[0:HALF]
        zpw[f, HALF:BLK] = z[ROWS - HALF:]
        a, b = split(z[HALF:ROWS - HALF])
        zwh[f * MID:(f + 1) * MID] = a
        zwl[f * MID:(f + 1) * MID] = b

    zonal_local(g_ref[...], five(*[jnp.where(low, from_right[i], from_left[i]) for i in range(3)]), store)

    def two(j):
        cols = pl.ds(pl.multiple_of(j * BLK, BLK), 2 * BLK)
        return fluxes(zh[:, cols], zl[:, cols], w, MID)

    first = slice(0, BLK)
    last = slice(COLS - BLK, COLS)
    start = fluxes(jnp.concatenate([zwh[...], zh[:, first]], axis=1),
                   jnp.concatenate([zwl[...], zl[:, first]], axis=1), w, MID)
    for q in range(2):
        carry[q] = start[q]

    def step(j, _):
        a = two(2 * j)
        b = two(2 * j + 1)
        merge(fo, pl.multiple_of(j * CW, BLK), carry, a, MID)
        merge(fo, pl.multiple_of(j * CW + BLK, BLK), a, b, MID)
        for q in range(2):
            carry[q] = b[q]
        return 0

    lax.fori_loop(0, NB // 2 - 1, step, 0, unroll=UNROLL_B)
    early = flux_copies(fo, e_out, n_out, HALF, MID, 0, COLS - CW, sem.at[0])
    for copy in early:
        copy.start()
    a = two(NB - 2)
    merge(fo, COLS - CW, carry, a, MID)
    end = fluxes(jnp.concatenate([zh[:, last], zwh[...]], axis=1),
                 jnp.concatenate([zl[:, last], zwl[...]], axis=1), w, MID)
    merge(fo, COLS - BLK, a, end, MID)
    late = flux_copies(fo, e_out, n_out, HALF, MID, COLS - CW, CW, sem.at[1])
    for copy in late:
        copy.start()
    for copy in early + late:
        copy.wait()


def edge_kernel(npieces, *refs):
    sel_ref, e_in, n_in, zp, zpw = refs[:5]
    pieces = refs[5:5 + npieces]
    gx, w_ref, e_out, n_out, zh, zl, fo, carry, sem = refs[5 + npieces:]
    sel = sel_ref[0]
    w = w_ref[...]
    zrow = pl.ds(pl.multiple_of(sel * HALF, HALF), HALF)
    orow = pl.multiple_of(sel * (ROWS - HALF), HALF)
    gmat = gx[sel]

    def zonal(piece, cols, part, pcols, stores):
        for f, x in enumerate(five(piece[0, :, cols], piece[1, :, cols], piece[2, :, cols])):
            hi, lo = split(x)
            z = part[f, zrow, pcols] + dot(gmat, jnp.concatenate([hi, lo, hi], axis=0))
            a, b = split(z)
            for s in stores:
                zh[f * HALF:(f + 1) * HALF, s] = a
                zl[f * HALF:(f + 1) * HALF, s] = b

    def two(p):
        cols = pl.ds(p * BLK, 2 * BLK)
        return fluxes(zh[:, cols], zl[:, cols], w, HALF)

    n = pieces[-1].shape[2]
    zonal(pieces[-1], slice(n - BLK, n), zpw, slice(0, BLK), [slice(0, BLK), slice(COLS + BLK, COLS + CW)])
    base = 0
    for piece in pieces:
        n = min(piece.shape[2], COLS - base)
        for c in range(0, n, EW):
            k = min(EW, n - c)
            zonal(piece, slice(c, c + k), zp, slice(base + c, base + c + k), [slice(base + c + BLK, base + c + k + BLK)])
        base += n
    left = two(0)
    for b in range(NB):
        right = two(b + 1)
        merge(fo, b * BLK, left, right, HALF)
        left = right
        if b == NB - 3:
            early = flux_copies(fo, e_out, n_out, orow, HALF, 0, COLS - CW, sem.at[0])
            for copy in early:
                copy.start()
    late = flux_copies(fo, e_out, n_out, orow, HALF, COLS - CW, CW, sem.at[1])
    for copy in late:
        copy.start()
    for copy in early + late:
        copy.wait()


ANY = pl.BlockSpec(memory_space=pl.ANY)
HBM = pl.BlockSpec(memory_space=pltpu.HBM)
VMEM = pl.BlockSpec(memory_space=pltpu.VMEM)
SMEM = pl.BlockSpec(memory_space=pltpu.SMEM)
COST = pl.CostEstimate(flops=1_000_000, bytes_accessed=1_000_000, transcendentals=0)
FLUX = jax.ShapeDtypeStruct((ROWS, COLS), F32)


def params(mib):
    return pltpu.CompilerParams(vmem_limit_bytes=mib * 2**20)


def lat_matrix():
    hi, lo = hi_lo(toeplitz(BLK, 2 * BLK, -HALF).T)
    return jnp.asarray(np.concatenate([hi, lo], axis=1))


def lon_matrix():
    hi, lo = hi_lo(toeplitz(ROWS, ROWS, 0))
    return jnp.asarray(np.concatenate([hi, lo], axis=0))


def halo_matrix():
    mats = []
    for shift in (-HALF, HALF):
        hi, lo = hi_lo(toeplitz(HALF, HALF, shift))
        mats.append(np.concatenate([hi, hi, lo], axis=1))
    return jnp.asarray(np.stack(mats))


def prep(core, u, v, t, m):
    side = jax.ShapeDtypeStruct((3, ROWS, BLK), F32)
    return pl.pallas_call(
        prep_kernel,
        out_shape=(jax.ShapeDtypeStruct((3, HALF, COLS), F32), side, side),
        in_specs=[SMEM] + [HBM] * 4,
        out_specs=(VMEM,) * 3,
        scratch_shapes=[
            pltpu.VMEM((3, HALF, COLS), F32),
            pltpu.VMEM((HALF, COLS), jnp.int32),
            pltpu.VMEM((2, 3, ROWS, BLK), F32),
            pltpu.VMEM((2, ROWS, BLK), jnp.int32),
            pltpu.SemaphoreType.DMA((3, 4)),
        ],
        compiler_params=params(PREP_MIB),
        cost_estimate=COST,
        name="prep",
    )(core, u, v, t, m)


def zonal(core, u, v, t, m):
    half = jax.ShapeDtypeStruct((5 * MID, COLS), BF)
    near = [jax.ShapeDtypeStruct((3, HALF, b - a), F32) for a, b in zip(NEAR[:-1], NEAR[1:])]
    return pl.pallas_call(
        zonal_kernel,
        out_shape=(half, half, jax.ShapeDtypeStruct((5, BLK, COLS), F32), *near),
        in_specs=[SMEM] + [HBM] * 4 + [VMEM],
        out_specs=(VMEM,) * (3 + len(near)),
        scratch_shapes=[
            pltpu.VMEM((ROWS, COLS), F32),
            pltpu.VMEM((ROWS, COLS), F32),
            pltpu.VMEM((ROWS, COLS), F32),
            pltpu.VMEM((ROWS, COLS), jnp.int32),
            pltpu.SemaphoreType.DMA((4, COLS // DW)),
        ],
        compiler_params=params(ZONAL_MIB),
        cost_estimate=COST,
        name="zonal",
    )(core, u, v, t, m, lon_matrix())


def middle(zh, zl, from_left, from_right):
    return pl.pallas_call(
        middle_kernel,
        out_shape=(FLUX, FLUX, jax.ShapeDtypeStruct((5, BLK, BLK), F32)),
        in_specs=[VMEM] * 6,
        out_specs=(ANY, ANY, VMEM),
        scratch_shapes=[
            pltpu.VMEM((5 * MID, BLK), BF),
            pltpu.VMEM((5 * MID, BLK), BF),
            pltpu.VMEM((2, MID, COLS), F32),
            pltpu.VMEM((2, MID, BLK), F32),
            pltpu.SemaphoreType.DMA((2, 2)),
        ],
        compiler_params=params(MID_MIB),
        cost_estimate=COST,
        name="middle",
    )(zh, zl, from_left, from_right, lon_matrix(), lat_matrix())


def edge(sel, east, north, zp, zpw, pieces, name):
    return pl.pallas_call(
        functools.partial(edge_kernel, len(pieces)),
        out_shape=(FLUX, FLUX),
        in_specs=[SMEM, ANY, ANY] + [VMEM] * (4 + len(pieces)),
        out_specs=(ANY, ANY),
        scratch_shapes=[
            pltpu.VMEM((5 * HALF, COLS + CW), BF),
            pltpu.VMEM((5 * HALF, COLS + CW), BF),
            pltpu.VMEM((2, HALF, COLS), F32),
            pltpu.VMEM((2, HALF, BLK), F32),
            pltpu.SemaphoreType.DMA((2, 2)),
        ],
        input_output_aliases={1: 0, 2: 1},
        compiler_params=params(EDGE_MIB),
        cost_estimate=COST,
        name=name,
    )(sel, east, north, zp, zpw, *pieces, halo_matrix(), lat_matrix())


def shards(u, v, t, m):
    nlon, nlat = lax.axis_size("lon"), lax.axis_size("lat")
    core = lax.axis_index("lon") % 2
    xoff = core * (ROWS - HALF)
    ioff = (1 - core) * (ROWS - HALF)
    across = [(i, (i + 1) % nlon if i % 2 else (i - 1) % nlon) for i in range(nlon)]
    inside = [(i, i + 1 - 2 * (i % 2)) for i in range(nlon)]
    up = [(i, i + 1) for i in range(nlat - 1)]
    down = [(j, i) for i, j in up]

    sel = core.astype(jnp.int32).reshape(1)
    u, v, t, m = (pltpu.with_memory_space_constraint(a, pltpu.HBM) for a in (u, v, t, m))
    x1, to_right, to_left = prep(sel, u, v, t, m)
    x1 = lax.ppermute(x1, "lon", across)
    from_left = lax.ppermute(to_right, "lat", up)
    from_right = lax.ppermute(to_left, "lat", down)
    zh, zl, zp, *near = zonal(sel, u, v, t, m)
    zh, zl, from_left, from_right = lax.optimization_barrier((zh, zl, from_left, from_right))
    lane = lax.broadcasted_iota(jnp.int32, (3, HALF, BLK), 2)

    def corner(row):
        def cut(a):
            return lax.dynamic_slice(a, (0, row, 0), (3, HALF, BLK))

        return jnp.where(lane < HALF, cut(from_right), cut(from_left))

    x2 = corner(xoff)
    near[-1] = jnp.concatenate([near[-1], corner(ioff)], axis=2)
    x2, near, zh, zl = lax.optimization_barrier((x2, near, zh, zl))
    x2 = lax.ppermute(x2, "lon", across)
    near = [lax.ppermute(part, "lon", inside) for part in near]
    east, north, zpw = middle(zh, zl, from_left, from_right)
    east, north = edge(1 - sel, east, north, zp, zpw, near, "edge_near")
    return edge(sel, east, north, zp, zpw, (x1, x2), "edge_far")


def solution(mesh):
    return jax.shard_map(
        shards,
        mesh=mesh,
        in_specs=(P("lon", "lat"),) * 4,
        out_specs=(P("lon", "lat"),) * 2,
        check_vma=False,
    )
```

time: 164 us -> 41.8 us (0.25); the launches traced: 162 us -> 41.7 us
  matrix products: 60 us -> 0 us
  other arithmetic: 35.6 us -> 0.07 us
  waiting for transfers between devices: 34 us -> 1.95 us
  Pallas kernels: 0 us -> 22.2 us
  local copies, waits for them, and re-layouts: 17.7 us -> 0.02 us
  starting transfers between devices: 12.6 us -> 16.5 us
    dot_general x4 -> x0, matrix products: 60 us -> none  [the longest x1 16.7 us: filter_lons(): jnp.einsum('ij,fbjr->fbir', weights_band[:, block_len:], trailing, precis...]
    ppermute x4 -> x7, waiting for transfers between devices: 34 us -> 1.95 us  [the longest x1 1.93 us: shards(): from_right = lax.ppermute(to_left, 'lat', down)]
    pallas_call x0 -> x5, Pallas kernels: none -> 22.2 us  [the longest x2 7.23 us: edge(): pl.pallas_call(functools.partial(edge_kernel, len(pieces)), out_shape=(FL...]
    concatenate x2 -> x1, other arithmetic: 19.4 us -> 0.04 us  [shards(): near[-1] = jnp.concatenate([near[-1], corner(ioff)], axis=2)]
    reshape x1 -> x0, local copies, waits for them, and re-layouts: 11.2 us -> none  [filter_lons(): return result.reshape(nfields, length, width)]
    unnamed x4 -> x0, other arithmetic: 6.63 us -> none
    mul x1 -> x0, other arithmetic: 6.4 us -> none  [heat_fluxes(): north = flux_scale * (filtered[4] - filtered[1] * filtered[2])]
    unnamed x12 -> x6, local copies, waits for them, and re-layouts: 4.71 us -> 0.02 us
  transfers between devices with their start and end apart: 4 -> 7, of which waited for: 3 -> 1; matrix products, arithmetic and copies ran while one was open for 2% -> 0% of each run, Pallas kernels for 0% -> 37%
where the time goes in v2:
time: 41.8 us; the launch traced here: 41.7 us
  Pallas kernels  22.2 us (53%)
  starting transfers between devices  16.5 us (39%)
  waiting for transfers between devices  1.95 us (5%)
  between operations  0.97 us (2%)
    pallas_call x2, Pallas kernels, edge(): pl.pallas_call(functools.partial(edge_kernel, len(pieces)), out_shape=(FL...  7.23 us
    pallas_call x1, Pallas kernels, zonal(): pl.pallas_call(zonal_kernel, out_shape=(half, half, jax.ShapeDtypeStruct(...  6.95 us
    ppermute x1, starting transfers between devices, shards(): from_left = lax.ppermute(to_right, 'lat', up)  5.03 us
    ppermute x1, starting transfers between devices, shards(): x1 = lax.ppermute(x1, 'lon', across)  4.97 us
    pallas_call x1, Pallas kernels, middle(): pl.pallas_call(middle_kernel, out_shape=(FLUX, FLUX, jax.ShapeDtypeStruct...  4.84 us
    ppermute x1, starting transfers between devices, shards(): x2 = lax.ppermute(x2, 'lon', across)  3.85 us
    pallas_call x1, Pallas kernels, prep(): pl.pallas_call(prep_kernel, out_shape=(jax.ShapeDtypeStruct((3, HALF, COL...  3.17 us
    ppermute x1, waiting for transfers between devices, shards(): from_right = lax.ppermute(to_left, 'lat', down)  1.93 us
  transfers between devices with their start and end apart: 7, of which 1 were waited for; matrix products, arithmetic and copies ran while one was open for 0% of the time, Pallas kernels for 37%

profile of v2, /device:TPU:96, one launch (start us, length us, event | category | flops | bytes accessed | tf_op | source)
XLA Modules:
  0.0 41.7 jit_solution(9912114837000209380)
XLA Ops:
  0.6 0.0 copy-start.1
  0.7 3.2 %prep.1 = (f32[3,64,2048]{2,1,0:T(8,128)}, f32[3,256,128]{2,1,0:T(8,128)S(1)}, f32[3,256,128]{2,1,0:T(8,128)S(1)}) custom-call(s32[1]{0:T(128)} %bitcast.core.refs_0_, f32[256,2048]{1,0:T(8,128)} %u.3, f32[256,2048]{1,0:T(8,128)} %v.3, f32[256,2048]{1,0:T(8,128)} %t.3, s32[256,2048]{1,0:T(8,128)} %m.3), custom_call_target="tpu_custom_call" | custom-call | flops 1000000 | bytes 1000000 | tf_op jit(solution)/shard_map/prep/pallas_call | solution.py:292
  3.8 5.0 %collective-permute-start.5 = (f32[3,64,2048]{2,1,0:T(8,128)}, f32[3,64,2048]{2,1,0:T(8,128)S(1)}, u32[]{:S(2)}, u32[]{:S(2)}) collective-permute-start(f32[3,64,2048]{2,1,0:T(8,128)} %get-tuple-element.48), channel_id=1, source_target_pairs={{0,240},{16,32},{32,16},{48,64},{64,48},{80,96},{96,80},{112,128},... | collective-permute-start | bytes 4718600 | tf_op jit(solution)/shard_map/ppermute | solution.py:383
  8.8 5.0 %collective-permute-start = (f32[3,256,128]{2,1,0:T(8,128)S(1)}, f32[3,256,128]{2,1,0:T(8,128)S(1)}, u32[]{:S(2)}, u32[]{:S(2)}) collective-permute-start(f32[3,256,128]{2,1,0:T(8,128)S(1)} %get-tuple-element.28), channel_id=1, source_target_pairs={{0,1},{1,2},{2,3},{3,4},{4,5},{5,6},{6,7},{7,8},{8,9},{9,10},{10,1... | collective-permute-start | bytes 1179656 | tf_op jit(solution)/shard_map/ppermute | solution.py:384
  13.8 1.9 %collective-permute-start.1 = (f32[3,256,128]{2,1,0:T(8,128)S(1)}, f32[3,256,128]{2,1,0:T(8,128)S(1)}, u32[]{:S(2)}, u32[]{:S(2)}) collective-permute-start(f32[3,256,128]{2,1,0:T(8,128)S(1)} %get-tuple-element.29), channel_id=1, source_target_pairs={{1,0},{2,1},{3,2},{4,3},{5,4},{6,5},{7,6},{8,7},{9,8},{10,9},{11,1... | collective-permute-start | bytes 1179656 | tf_op jit(solution)/shard_map/ppermute | solution.py:385
  15.8 0.0 copy-done.1
  15.8 0.0 copy-start
  15.8 7.0 %zonal.1 = (bf16[640,2048]{1,0:T(8,128)(2,1)S(1)}, bf16[640,2048]{1,0:T(8,128)(2,1)S(1)}, f32[5,128,2048]{2,1,0:T(8,128)S(1)}, f32[3,64,768]{2,1,0:T(8,128)S(1)}...) custom-call(s32[1]{0:T(128)} %bitcast.core.refs_0_, f32[256,2048]{1,0:T(8,128)} %u.3, f32[256,2048]{1,0:T(8,128)} %v.3, ...), custom_call_target="tpu_custom_call" | custom-call | flops 1000000 | bytes 1000000 | tf_op jit(solution)/shard_map/zonal/pallas_call | solution.py:313
  22.8 0.0 collective-permute-done.from_left
  22.8 1.9 %collective-permute-done.1.from_right = f32[3,256,128]{2,1,0:T(8,128)S(1)} collective-permute-done((f32[3,256,128]{2,1,0:T(8,128)S(1)}, f32[3,256,128]{2,1,0:T(8,128)S(1)}, u32[]{:S(2)}, u32[]{:S(2)}) %collective-permute-start.1) | collective-permute-done | bytes 393248 | tf_op jit(solution)/shard_map/ppermute | solution.py:385
  24.8 0.1 collective-permute-start.2
  24.9 0.5 %collective-permute-start.3 = (f32[3,64,768]{2,1,0:T(8,128)S(1)}, f32[3,64,768]{2,1,0:T(8,128)S(1)}, u32[]{:S(2)}, u32[]{:S(2)}) collective-permute-start(f32[3,64,768]{2,1,0:T(8,128)S(1)} %get-tuple-element.44), channel_id=1, source_target_pairs={{0,16},{16,0},{32,48},{48,32},{64,80},{80,64},{96,112},{112,96},{1... | collective-permute-start | bytes 1769480 | tf_op jit(solution)/shard_map/ppermute | solution.py:400
  25.4 0.1 collective-permute-start.4
  25.5 3.8 %collective-permute-start.6 = (f32[3,64,128]{2,1,0:T(8,128)S(1)}, f32[3,64,128]{2,1,0:T(8,128)S(1)}, u32[]{:S(2)}, u32[]{:S(2)}) collective-permute-start(f32[3,64,128]{2,1,0:T(8,128)S(1)} %get-tuple-element.49), channel_id=1, source_target_pairs={{0,240},{16,32},{32,16},{48,64},{64,48},{80,96},{96,80},{112,128},... | collective-permute-start | bytes 294920 | tf_op jit(solution)/shard_map/ppermute | solution.py:399
  29.3 0.0 copy-done
  29.3 4.8 %middle.1 = (f32[256,2048]{1,0:T(8,128)}, f32[256,2048]{1,0:T(8,128)}, f32[5,128,128]{2,1,0:T(8,128)S(1)}) custom-call(bf16[640,2048]{1,0:T(8,128)(2,1)S(1)} %get-tuple-element.37.zh, bf16[640,2048]{1,0:T(8,128)(2,1)S(1)} %get-tuple-element.38.zl, f32[3,256,128]{2,1,0:T(8,128)S(1)} %collective-permute-done.from_left, ...), custom_call_target="tpu_custom_call" | custom-call | flops 1000000 | bytes 1000000 | tf_op jit(solution)/shard_map/middle/pallas_call | solution.py:332
  34.2 0.0 collective-permute-done.4.refs_7_
  34.2 0.0 collective-permute-done.2.refs_5_
  34.2 0.0 collective-permute-done.3.refs_6_
  34.2 0.0 copy-done.2
  34.2 3.6 %edge_near.1 = (f32[256,2048]{1,0:T(8,128)}, f32[256,2048]{1,0:T(8,128)}) custom-call(s32[1]{0:T(128)S(6)} %sub.6.refs_0_, f32[256,2048]{1,0:T(8,128)} %get-tuple-element.39.refs_1_, f32[256,2048]{1,0:T(8,128)} %get-tuple-element.40.refs_2_, f32[5,128,2048]{2,1,0:T(8,128)S(1)} %get-tuple-element.41.refs_3_, ...), custom_call_target="tpu_custom_call", output_to_operand_aliasing={{0}: (1, {}), {1}: (2, {})} | custom-call | flops 1000000 | bytes 1000000 | tf_op jit(solution)/shard_map/edge_near/pallas_call | solution.py:351
  37.9 0.0 collective-permute-done.6.refs_6_
  37.9 0.0 collective-permute-done.5.refs_5_
  37.9 3.6 %edge_far.1 = (f32[256,2048]{1,0:T(8,128)}, f32[256,2048]{1,0:T(8,128)}) custom-call(s32[1]{0:T(128)} %bitcast.core.refs_0_, f32[256,2048]{1,0:T(8,128)} %get-tuple-element.46.refs_1_, f32[256,2048]{1,0:T(8,128)} %get-tuple-element.47.refs_2_, f32[5,128,2048]{2,1,0:T(8,128)S(1)} %get-tuple-element.41.refs_3_, ...), custom_call_target="tpu_custom_call", output_to_operand_aliasing={{0}: (1, {}), {1}: (2, {})} | custom-call | flops 1000000 | bytes 1000000 | tf_op jit(solution)/shard_map/edge_far/pallas_call | solution.py:351
  (4 shorter events, 0.1 us)
Async XLA Ops:
  0.6 15.1 %copy-start.1 = (bf16[512,256]{1,0:T(8,128)(2,1)S(1)}, bf16[512,256]{1,0:T(8,128)(2,1)}, u32[]{:S(2)}) copy-start(bf16[512,256]{1,0:T(8,128)(2,1)} %constant.34.clone.g_ref) | copy-start | bytes 786436
  3.8 34.0 %collective-permute-start.5 = (f32[3,64,2048]{2,1,0:T(8,128)}, f32[3,64,2048]{2,1,0:T(8,128)S(1)}, u32[]{:S(2)}, u32[]{:S(2)}) collective-permute-start(f32[3,64,2048]{2,1,0:T(8,128)} %get-tuple-element.48), channel_id=1, source_target_pairs={{0,240},{16,32},{32,16},{48,64},{64,48},{80,96},{96,80},{112,128},... | collective-permute-start | bytes 4718600 | tf_op jit(solution)/shard_map/ppermute | solution.py:383
  8.8 14.0 %collective-permute-start = (f32[3,256,128]{2,1,0:T(8,128)S(1)}, f32[3,256,128]{2,1,0:T(8,128)S(1)}, u32[]{:S(2)}, u32[]{:S(2)}) collective-permute-start(f32[3,256,128]{2,1,0:T(8,128)S(1)} %get-tuple-element.28), channel_id=1, source_target_pairs={{0,1},{1,2},{2,3},{3,4},{4,5},{5,6},{6,7},{7,8},{8,9},{9,10},{10,1... | collective-permute-start | bytes 1179656 | tf_op jit(solution)/shard_map/ppermute | solution.py:384
  13.8 10.9 %collective-permute-start.1 = (f32[3,256,128]{2,1,0:T(8,128)S(1)}, f32[3,256,128]{2,1,0:T(8,128)S(1)}, u32[]{:S(2)}, u32[]{:S(2)}) collective-permute-start(f32[3,256,128]{2,1,0:T(8,128)S(1)} %get-tuple-element.29), channel_id=1, source_target_pairs={{1,0},{2,1},{3,2},{4,3},{5,4},{6,5},{7,6},{8,7},{9,8},{10,9},{11,1... | collective-permute-start | bytes 1179656 | tf_op jit(solution)/shard_map/ppermute | solution.py:385
  15.8 13.5 %copy-start = (bf16[256,256]{1,0:T(8,128)(2,1)S(1)}, bf16[256,256]{1,0:T(8,128)(2,1)}, u32[]{:S(2)}) copy-start(bf16[256,256]{1,0:T(8,128)(2,1)} %constant.35.clone.w_ref.refs_9_.refs_8_) | copy-start | bytes 393220
  24.8 9.4 %collective-permute-start.2 = (f32[3,64,768]{2,1,0:T(8,128)S(1)}, f32[3,64,768]{2,1,0:T(8,128)S(1)}, u32[]{:S(2)}, u32[]{:S(2)}) collective-permute-start(f32[3,64,768]{2,1,0:T(8,128)S(1)} %get-tuple-element.43), channel_id=1, source_target_pairs={{0,16},{16,0},{32,48},{48,32},{64,80},{80,64},{96,112},{112,96},{1... | collective-permute-start | bytes 1769480 | tf_op jit(solution)/shard_map/ppermute | solution.py:400
  24.9 9.3 %collective-permute-start.3 = (f32[3,64,768]{2,1,0:T(8,128)S(1)}, f32[3,64,768]{2,1,0:T(8,128)S(1)}, u32[]{:S(2)}, u32[]{:S(2)}) collective-permute-start(f32[3,64,768]{2,1,0:T(8,128)S(1)} %get-tuple-element.44), channel_id=1, source_target_pairs={{0,16},{16,0},{32,48},{48,32},{64,80},{80,64},{96,112},{112,96},{1... | collective-permute-start | bytes 1769480 | tf_op jit(solution)/shard_map/ppermute | solution.py:400
  25.4 8.8 %collective-permute-start.4 = (f32[3,64,640]{2,1,0:T(8,128)S(1)}, f32[3,64,640]{2,1,0:T(8,128)S(1)}, u32[]{:S(2)}, u32[]{:S(2)}) collective-permute-start(f32[3,64,640]{2,1,0:T(8,128)S(1)} %pad_maximum_fusion), channel_id=1, source_target_pairs={{0,16},{16,0},{32,48},{48,32},{64,80},{80,64},{96,112},{112,96},{1... | collective-permute-start | bytes 1474568 | tf_op jit(solution)/shard_map/ppermute | solution.py:400
  25.5 12.4 %collective-permute-start.6 = (f32[3,64,128]{2,1,0:T(8,128)S(1)}, f32[3,64,128]{2,1,0:T(8,128)S(1)}, u32[]{:S(2)}, u32[]{:S(2)}) collective-permute-start(f32[3,64,128]{2,1,0:T(8,128)S(1)} %get-tuple-element.49), channel_id=1, source_target_pairs={{0,240},{16,32},{32,16},{48,64},{64,48},{80,96},{96,80},{112,128},... | collective-permute-start | bytes 294920 | tf_op jit(solution)/shard_map/ppermute | solution.py:399
  29.3 4.9 %copy-start.2 = (bf16[2,64,192]{2,1,0:T(8,128)(2,1)S(1)}, bf16[2,64,192]{2,1,0:T(8,128)(2,1)}, u32[]{:S(2)}) copy-start(bf16[2,64,192]{2,1,0:T(8,128)(2,1)} %constant.36.clone.refs_8_.refs_7_) | copy-start | bytes 147460

commit v3 on v2

--- a/solution.py
+++ b/solution.py
@@ -19,6 +19,7 @@
 MID = ROWS - BLK
 EW = 512
 DW = 512
+AHEAD = 2
 NEAR = (0, 768, 1536, COLS)
 PREP_MIB = 8
 MID_MIB = 6
@@ -87,12 +88,13 @@
         store(f, r[:ROWS] + r[ROWS:] + dot(g[:ROWS], lo))
 
 
-def prep_kernel(core, u, v, t, m, x1, to_right, to_left, rows, wet_rows, cols, wet_cols, sem):
-    top = pl.ds(pl.multiple_of(core[0] * (ROWS - HALF), HALF), HALF)
-    sides = (pl.ds(COLS - BLK, BLK), pl.ds(0, BLK))
+def prep_kernel(where, u, v, t, m, x1, first, second, rows, wet_rows, cols, wet_cols, sem):
+    top = pl.ds(pl.multiple_of(where[0] * (ROWS - HALF), HALF), HALF)
+    odd = where[1]
     copies = [pltpu.make_async_copy(m.at[top, :], wet_rows, sem.at[0, 3])]
     copies += [pltpu.make_async_copy(a.at[top, :], rows.at[i], sem.at[0, i]) for i, a in enumerate((u, v, t))]
-    for s, side in enumerate(sides):
+    for s, near_end in enumerate((odd, 1 - odd)):
+        side = pl.ds(pl.multiple_of((1 - near_end) * (COLS - BLK), BLK), BLK)
         copies.append(pltpu.make_async_copy(m.at[:, side], wet_cols.at[s], sem.at[1 + s, 3]))
         copies += [pltpu.make_async_copy(a.at[:, side], cols.at[s, i], sem.at[1 + s, i])
                    for i, a in enumerate((u, v, t))]
@@ -103,12 +105,37 @@
     wet = wet_rows[...].astype(F32)
     for i in range(3):
         x1[i] = wet * rows[i]
-    for s, out in enumerate((to_right, to_left)):
+    low = lax.broadcasted_iota(jnp.int32, (BLK, BLK), 1) < HALF
+    for s, (out, near_end) in enumerate(((first, odd), (second, 1 - odd))):
         for copy in copies[4 + 4 * s:8 + 4 * s]:
             copy.wait()
         wet = wet_cols[s].astype(F32)
         for i in range(3):
-            out[i] = wet * cols[s, i]
+            x = wet * cols[s, i]
+            y = pltpu.roll(x, HALF, 1)
+            out[i] = jnp.where(
+                near_end == 1,
+                jnp.where(low, x[:BLK], y[BLK:]),
+                jnp.where(low, y[:BLK], x[BLK:]),
+            )
+
+
+def corner_kernel(where, first, second, main, wrap, far, near):
+    lower = where[0] == 0
+    even = where[1] == 0
+    low = lax.broadcasted_iota(jnp.int32, (BLK, BLK), 1) < HALF
+    width = main.shape[2]
+    near[:, :, 0:width] = main[...]
+    for i in range(3):
+        a, b = first[i], second[i]
+        right = jnp.where(even, a, b)
+        left = jnp.where(even, b, a)
+        top = jnp.where(low, right, pltpu.roll(left, HALF, 1))
+        bottom = jnp.where(low, pltpu.roll(right, HALF, 1), left)
+        wrap[i, 0:BLK] = top
+        wrap[i, BLK:ROWS] = bottom
+        far[i] = jnp.where(lower, top[:HALF], bottom[HALF:])
+        near[i, :, width:width + BLK] = jnp.where(lower, bottom[HALF:], top[:HALF])
 
 
 def zonal_kernel(core, u, v, t, m, g_ref, zh, zl, zp, *refs):
@@ -123,7 +150,7 @@
             for i, (src, dst) in enumerate(((u, ub), (v, vb), (t, tb), (m, mb)))
         ]
 
-    for j in range(2):
+    for j in range(AHEAD):
         for copy in copies(j):
             copy.start()
     for j in range(COLS // CW):
@@ -131,8 +158,8 @@
             k = j * CW // DW
             for copy in copies(k):
                 copy.wait()
-            if k + 2 < COLS // DW:
-                for copy in copies(k + 2):
+            if k + AHEAD < COLS // DW:
+                for copy in copies(k + AHEAD):
                     copy.start()
         cols = pl.ds(j * CW, CW)
         wet = mb[:, cols].astype(F32)
@@ -159,10 +186,9 @@
     ]
 
 
-def middle_kernel(zh, zl, from_left, from_right, g_ref, w_ref, e_out, n_out, zpw,
+def middle_kernel(zh, zl, wrap, g_ref, w_ref, e_out, n_out, zpw,
                   zwh, zwl, fo, carry, sem):
     w = w_ref[...]
-    low = lax.broadcasted_iota(jnp.int32, (ROWS, BLK), 1) < HALF
 
     def store(f, z):
         zpw[f, 0:HALF] = z[0:HALF]
@@ -171,7 +197,7 @@
         zwh[f * MID:(f + 1) * MID] = a
         zwl[f * MID:(f + 1) * MID] = b
 
-    zonal_local(g_ref[...], five(*[jnp.where(low, from_right[i], from_left[i]) for i in range(3)]), store)
+    zonal_local(g_ref[...], five(wrap[0], wrap[1], wrap[2]), store)
 
     def two(j):
         cols = pl.ds(pl.multiple_of(j * BLK, BLK), 2 * BLK)
@@ -288,7 +314,7 @@
 
 
 def prep(core, u, v, t, m):
-    side = jax.ShapeDtypeStruct((3, ROWS, BLK), F32)
+    side = jax.ShapeDtypeStruct((3, BLK, BLK), F32)
     return pl.pallas_call(
         prep_kernel,
         out_shape=(jax.ShapeDtypeStruct((3, HALF, COLS), F32), side, side),
@@ -305,6 +331,22 @@
         cost_estimate=COST,
         name="prep",
     )(core, u, v, t, m)
+
+
+def corners(where, first, second, main):
+    return pl.pallas_call(
+        corner_kernel,
+        out_shape=(
+            jax.ShapeDtypeStruct((3, ROWS, BLK), F32),
+            jax.ShapeDtypeStruct((3, HALF, BLK), F32),
+            jax.ShapeDtypeStruct((3, HALF, main.shape[2] + BLK), F32),
+        ),
+        in_specs=[SMEM] + [VMEM] * 3,
+        out_specs=(VMEM,) * 3,
+        compiler_params=params(2),
+        cost_estimate=COST,
+        name="corners",
+    )(where, first, second, main)
 
 
 def zonal(core, u, v, t, m):
@@ -328,11 +370,11 @@
     )(core, u, v, t, m, lon_matrix())
 
 
-def middle(zh, zl, from_left, from_right):
+def middle(zh, zl, wrap):
     return pl.pallas_call(
         middle_kernel,
         out_shape=(FLUX, FLUX, jax.ShapeDtypeStruct((5, BLK, BLK), F32)),
-        in_specs=[VMEM] * 6,
+        in_specs=[VMEM] * 5,
         out_specs=(ANY, ANY, VMEM),
         scratch_shapes=[
             pltpu.VMEM((5 * MID, BLK), BF),
@@ -344,7 +386,7 @@
         compiler_params=params(MID_MIB),
         cost_estimate=COST,
         name="middle",
-    )(zh, zl, from_left, from_right, lon_matrix(), lat_matrix())
+    )(zh, zl, wrap, lon_matrix(), lat_matrix())
 
 
 def edge(sel, east, north, zp, zpw, pieces, name):
@@ -370,35 +412,26 @@
 def shards(u, v, t, m):
     nlon, nlat = lax.axis_size("lon"), lax.axis_size("lat")
     core = lax.axis_index("lon") % 2
-    xoff = core * (ROWS - HALF)
-    ioff = (1 - core) * (ROWS - HALF)
     across = [(i, (i + 1) % nlon if i % 2 else (i - 1) % nlon) for i in range(nlon)]
     inside = [(i, i + 1 - 2 * (i % 2)) for i in range(nlon)]
-    up = [(i, i + 1) for i in range(nlat - 1)]
-    down = [(j, i) for i, j in up]
+    odd = lax.axis_index("lat") % 2
+    even_pairs = [(i, i + 1 - 2 * (i % 2)) for i in range(nlat)]
+    odd_pairs = [(i, i - 1 + 2 * (i % 2)) for i in range(1, nlat - 1)]
 
     sel = core.astype(jnp.int32).reshape(1)
     u, v, t, m = (pltpu.with_memory_space_constraint(a, pltpu.HBM) for a in (u, v, t, m))
-    x1, to_right, to_left = prep(sel, u, v, t, m)
+    where = jnp.stack([core, odd]).astype(jnp.int32)
+    x1, first, second = prep(where, u, v, t, m)
     x1 = lax.ppermute(x1, "lon", across)
-    from_left = lax.ppermute(to_right, "lat", up)
-    from_right = lax.ppermute(to_left, "lat", down)
+    first = lax.ppermute(first, "lat", even_pairs)
+    second = lax.ppermute(second, "lat", odd_pairs)
     zh, zl, zp, *near = zonal(sel, u, v, t, m)
-    zh, zl, from_left, from_right = lax.optimization_barrier((zh, zl, from_left, from_right))
-    lane = lax.broadcasted_iota(jnp.int32, (3, HALF, BLK), 2)
-
-    def corner(row):
-        def cut(a):
-            return lax.dynamic_slice(a, (0, row, 0), (3, HALF, BLK))
-
-        return jnp.where(lane < HALF, cut(from_right), cut(from_left))
-
-    x2 = corner(xoff)
-    near[-1] = jnp.concatenate([near[-1], corner(ioff)], axis=2)
+    zh, zl, first, second = lax.optimization_barrier((zh, zl, first, second))
+    wrap, x2, near[-1] = corners(where, first, second, near[-1])
     x2, near, zh, zl = lax.optimization_barrier((x2, near, zh, zl))
     x2 = lax.ppermute(x2, "lon", across)
     near = [lax.ppermute(part, "lon", inside) for part in near]
-    east, north, zpw = middle(zh, zl, from_left, from_right)
+    east, north, zpw = middle(zh, zl, wrap)
     east, north = edge(1 - sel, east, north, zp, zpw, near, "edge_near")
     return edge(sel, east, north, zp, zpw, (x1, x2), "edge_far")
 

time: 41.8 us -> 39.5 us (0.945)
  the two profiles are of different devices: /device:TPU:96 before, /device:TPU:31 now
where the time goes in v3:
time: 39.5 us; the launch traced here: 39.3 us
  Pallas kernels  22.4 us (57%)
  starting transfers between devices  15.9 us (40%)
  between operations  0.93 us (2%)
    pallas_call x2, Pallas kernels, edge(): pl.pallas_call(functools.partial(edge_kernel, len(pieces)), out_shape=(FL...  7.26 us
    pallas_call x1, Pallas kernels, zonal(): pl.pallas_call(zonal_kernel, out_shape=(half, half, jax.ShapeDtypeStruct(...  6.93 us
    ppermute x1, starting transfers between devices, shards(): second = lax.ppermute(second, 'lat', odd_pairs)  6.07 us
    ppermute x1, starting transfers between devices, shards(): x2 = lax.ppermute(x2, 'lon', across)  5.2 us
    pallas_call x1, Pallas kernels, middle(): pl.pallas_call(middle_kernel, out_shape=(FLUX, FLUX, jax.ShapeDtypeStruct...  4.83 us
    pallas_call x1, Pallas kernels, prep(): pl.pallas_call(prep_kernel, out_shape=(jax.ShapeDtypeStruct((3, HALF, COL...  2.67 us
    ppermute x1, starting transfers between devices, shards(): first = lax.ppermute(first, 'lat', even_pairs)  1.63 us
    ppermute x3, starting transfers between devices, shards(): near = [lax.ppermute(part, 'lon', inside) for part in near]  1.51 us
  transfers between devices with their start and end apart: 7, of which 0 were waited for; matrix products, arithmetic and copies ran while one was open for 0% of the time, Pallas kernels for 41%

profile of v3, /device:TPU:31, one launch (start us, length us, event | category | flops | bytes accessed | tf_op | source)
XLA Modules:
  0.0 39.3 jit_solution(5010768214124657564)
XLA Ops:
  0.6 0.1 pad_add_fusion.where
  0.7 2.7 %prep.1 = (f32[3,64,2048]{2,1,0:T(8,128)S(1)}, f32[3,128,128]{2,1,0:T(8,128)S(1)}, f32[3,128,128]{2,1,0:T(8,128)S(1)}) custom-call(s32[2]{0:T(128)S(1)} %pad_add_fusion.where, f32[256,2048]{1,0:T(8,128)} %u.3, f32[256,2048]{1,0:T(8,128)} %v.3, f32[256,2048]{1,0:T(8,128)} %t.3, s32[256,2048]{1,0:T(8,128)} %m.3), custom_call_target="tpu_custom_call" | custom-call | flops 1000000 | bytes 1000000 | tf_op jit(solution)/shard_map/prep/pallas_call | solution.py:318
  3.4 1.5 %collective-permute-start.5 = (f32[3,64,2048]{2,1,0:T(8,128)S(1)}, f32[3,64,2048]{2,1,0:T(8,128)S(1)}, u32[]{:S(2)}, u32[]{:S(2)}) collective-permute-start(f32[3,64,2048]{2,1,0:T(8,128)S(1)} %get-tuple-element.54), channel_id=1, source_target_pairs={{0,240},{16,32},{32,16},{48,64},{64,48},{80,96},{96,80},{112,128},... | collective-permute-start | bytes 4718600 | tf_op jit(solution)/shard_map/ppermute | solution.py:425
  4.9 1.6 %collective-permute-start = (f32[3,128,128]{2,1,0:T(8,128)S(1)}, f32[3,128,128]{2,1,0:T(8,128)S(1)}, u32[]{:S(2)}, u32[]{:S(2)}) collective-permute-start(f32[3,128,128]{2,1,0:T(8,128)S(1)} %get-tuple-element.31), channel_id=1, source_target_pairs={{0,1},{1,0},{2,3},{3,2},{4,5},{5,4},{6,7},{7,6},{8,9},{9,8},{10,11... | collective-permute-start | bytes 589832 | tf_op jit(solution)/shard_map/ppermute | solution.py:426
  6.5 6.1 %collective-permute-start.1 = (f32[3,128,128]{2,1,0:T(8,128)S(1)}, f32[3,128,128]{2,1,0:T(8,128)S(1)}, u32[]{:S(2)}, u32[]{:S(2)}) collective-permute-start(f32[3,128,128]{2,1,0:T(8,128)S(1)} %get-tuple-element.32), channel_id=1, source_target_pairs={{1,2},{2,1},{3,4},{4,3},{5,6},{6,5},{7,8},{8,7},{9,10},{10,9},{11,... | collective-permute-start | bytes 589832 | tf_op jit(solution)/shard_map/ppermute | solution.py:427
  12.6 0.0 copy-done.1
  12.6 6.9 %zonal.1 = (bf16[640,2048]{1,0:T(8,128)(2,1)S(1)}, bf16[640,2048]{1,0:T(8,128)(2,1)S(1)}, f32[5,128,2048]{2,1,0:T(8,128)S(1)}, f32[3,64,768]{2,1,0:T(8,128)S(1)}...) custom-call(s32[1]{0:T(128)} %bitcast.core.refs_0_, f32[256,2048]{1,0:T(8,128)} %u.3, f32[256,2048]{1,0:T(8,128)} %v.3, ...), custom_call_target="tpu_custom_call" | custom-call | flops 1000000 | bytes 1000000 | tf_op jit(solution)/shard_map/zonal/pallas_call | solution.py:355
  19.5 0.0 collective-permute-done.first
  19.6 0.0 collective-permute-done.1.second
  19.6 0.7 %corners.1 = (f32[3,256,128]{2,1,0:T(8,128)S(1)}, f32[3,64,128]{2,1,0:T(8,128)S(1)}, f32[3,64,640]{2,1,0:T(8,128)S(1)}) custom-call(s32[2]{0:T(128)S(1)} %pad_add_fusion.where, f32[3,128,128]{2,1,0:T(8,128)S(1)} %collective-permute-done.first, f32[3,128,128]{2,1,0:T(8,128)S(1)} %collective-permute-done.1.second, f32[3,64,512]{2,1,0:T(8,128)S(1)} %get-tuple-element.35.main), custom_call_target="tpu_custom_call" | custom-call | flops 1000000 | bytes 1000000 | tf_op jit(solution)/shard_map/corners/pallas_call | solution.py:337
  20.3 1.0 %collective-permute-start.2 = (f32[3,64,768]{2,1,0:T(8,128)S(1)}, f32[3,64,768]{2,1,0:T(8,128)S(1)}, u32[]{:S(2)}, u32[]{:S(2)}) collective-permute-start(f32[3,64,768]{2,1,0:T(8,128)S(1)} %get-tuple-element.49), channel_id=1, source_target_pairs={{0,16},{16,0},{32,48},{48,32},{64,80},{80,64},{96,112},{112,96},{1... | collective-permute-start | bytes 1769480 | tf_op jit(solution)/shard_map/ppermute | solution.py:433
  21.3 0.1 collective-permute-start.3
  21.4 0.4 %collective-permute-start.4 = (f32[3,64,640]{2,1,0:T(8,128)S(1)}, f32[3,64,640]{2,1,0:T(8,128)S(1)}, u32[]{:S(2)}, u32[]{:S(2)}) collective-permute-start(f32[3,64,640]{2,1,0:T(8,128)S(1)} %get-tuple-element.51), channel_id=1, source_target_pairs={{0,16},{16,0},{32,48},{48,32},{64,80},{80,64},{96,112},{112,96},{1... | collective-permute-start | bytes 1474568 | tf_op jit(solution)/shard_map/ppermute | solution.py:433
  21.8 5.2 %collective-permute-start.6 = (f32[3,64,128]{2,1,0:T(8,128)S(1)}, f32[3,64,128]{2,1,0:T(8,128)S(1)}, u32[]{:S(2)}, u32[]{:S(2)}) collective-permute-start(f32[3,64,128]{2,1,0:T(8,128)S(1)} %get-tuple-element.55), channel_id=1, source_target_pairs={{0,240},{16,32},{32,16},{48,64},{64,48},{80,96},{96,80},{112,128},... | collective-permute-start | bytes 294920 | tf_op jit(solution)/shard_map/ppermute | solution.py:432
  27.0 0.0 copy-done
  27.0 4.8 %middle.1 = (f32[256,2048]{1,0:T(8,128)}, f32[256,2048]{1,0:T(8,128)}, f32[5,128,128]{2,1,0:T(8,128)S(1)}) custom-call(bf16[640,2048]{1,0:T(8,128)(2,1)S(1)} %get-tuple-element.42.zh, bf16[640,2048]{1,0:T(8,128)(2,1)S(1)} %get-tuple-element.43.zl, f32[3,256,128]{2,1,0:T(8,128)S(1)} %get-tuple-element.44.wrap, bf16[512,256]{1,0:T(8,128)(2,1)S(1)} %copy-done.1, ...), custom_call_target="tpu_custom_call" | custom-call | flops 1000000 | bytes 1000000 | tf_op jit(solution)/shard_map/middle/pallas_call | solution.py:374
  31.8 0.0 collective-permute-done.4.refs_7_
  31.9 0.0 collective-permute-done.2.refs_5_
  31.9 0.0 collective-permute-done.3.refs_6_
  31.9 0.0 copy-done.2
  31.9 3.6 %edge_near.1 = (f32[256,2048]{1,0:T(8,128)}, f32[256,2048]{1,0:T(8,128)}) custom-call(s32[1]{0:T(128)S(6)} %sub.3.refs_0_, f32[256,2048]{1,0:T(8,128)} %get-tuple-element.45.refs_1_, f32[256,2048]{1,0:T(8,128)} %get-tuple-element.46.refs_2_, f32[5,128,2048]{2,1,0:T(8,128)S(1)} %get-tuple-element.47.refs_3_, ...), custom_call_target="tpu_custom_call", output_to_operand_aliasing={{0}: (1, {}), {1}: (2, {})} | custom-call | flops 1000000 | bytes 1000000 | tf_op jit(solution)/shard_map/edge_near/pallas_call | solution.py:393
  35.5 0.0 collective-permute-done.6.refs_6_
  35.5 0.0 collective-permute-done.5.refs_5_
  35.5 3.6 %edge_far.1 = (f32[256,2048]{1,0:T(8,128)}, f32[256,2048]{1,0:T(8,128)}) custom-call(s32[1]{0:T(128)} %bitcast.core.refs_0_, f32[256,2048]{1,0:T(8,128)} %get-tuple-element.52.refs_1_, f32[256,2048]{1,0:T(8,128)} %get-tuple-element.53.refs_2_, f32[5,128,2048]{2,1,0:T(8,128)S(1)} %get-tuple-element.47.refs_3_, ...), custom_call_target="tpu_custom_call", output_to_operand_aliasing={{0}: (1, {}), {1}: (2, {})} | custom-call | flops 1000000 | bytes 1000000 | tf_op jit(solution)/shard_map/edge_far/pallas_call | solution.py:393
  (3 shorter events, 0.0 us)
Async XLA Ops:
  0.7 11.9 %copy-start.1 = (bf16[512,256]{1,0:T(8,128)(2,1)S(1)}, bf16[512,256]{1,0:T(8,128)(2,1)}, u32[]{:S(2)}) copy-start(bf16[512,256]{1,0:T(8,128)(2,1)} %constant.32.clone.g_ref) | copy-start | bytes 786436
  3.4 32.1 %collective-permute-start.5 = (f32[3,64,2048]{2,1,0:T(8,128)S(1)}, f32[3,64,2048]{2,1,0:T(8,128)S(1)}, u32[]{:S(2)}, u32[]{:S(2)}) collective-permute-start(f32[3,64,2048]{2,1,0:T(8,128)S(1)} %get-tuple-element.54), channel_id=1, source_target_pairs={{0,240},{16,32},{32,16},{48,64},{64,48},{80,96},{96,80},{112,128},... | collective-permute-start | bytes 4718600 | tf_op jit(solution)/shard_map/ppermute | solution.py:425
  4.9 14.7 %collective-permute-start = (f32[3,128,128]{2,1,0:T(8,128)S(1)}, f32[3,128,128]{2,1,0:T(8,128)S(1)}, u32[]{:S(2)}, u32[]{:S(2)}) collective-permute-start(f32[3,128,128]{2,1,0:T(8,128)S(1)} %get-tuple-element.31), channel_id=1, source_target_pairs={{0,1},{1,0},{2,3},{3,2},{4,5},{5,4},{6,7},{7,6},{8,9},{9,8},{10,11... | collective-permute-start | bytes 589832 | tf_op jit(solution)/shard_map/ppermute | solution.py:426
  6.5 20.5 %copy-start = (bf16[256,256]{1,0:T(8,128)(2,1)S(1)}, bf16[256,256]{1,0:T(8,128)(2,1)}, u32[]{:S(2)}) copy-start(bf16[256,256]{1,0:T(8,128)(2,1)} %constant.33.clone.w_ref.refs_9_.refs_8_) | copy-start | bytes 393220
  6.5 13.0 %collective-permute-start.1 = (f32[3,128,128]{2,1,0:T(8,128)S(1)}, f32[3,128,128]{2,1,0:T(8,128)S(1)}, u32[]{:S(2)}, u32[]{:S(2)}) collective-permute-start(f32[3,128,128]{2,1,0:T(8,128)S(1)} %get-tuple-element.32), channel_id=1, source_target_pairs={{1,2},{2,1},{3,4},{4,3},{5,6},{6,5},{7,8},{8,7},{9,10},{10,9},{11,... | collective-permute-start | bytes 589832 | tf_op jit(solution)/shard_map/ppermute | solution.py:427
  20.3 11.6 %collective-permute-start.2 = (f32[3,64,768]{2,1,0:T(8,128)S(1)}, f32[3,64,768]{2,1,0:T(8,128)S(1)}, u32[]{:S(2)}, u32[]{:S(2)}) collective-permute-start(f32[3,64,768]{2,1,0:T(8,128)S(1)} %get-tuple-element.49), channel_id=1, source_target_pairs={{0,16},{16,0},{32,48},{48,32},{64,80},{80,64},{96,112},{112,96},{1... | collective-permute-start | bytes 1769480 | tf_op jit(solution)/shard_map/ppermute | solution.py:433
  21.3 10.6 %collective-permute-start.3 = (f32[3,64,768]{2,1,0:T(8,128)S(1)}, f32[3,64,768]{2,1,0:T(8,128)S(1)}, u32[]{:S(2)}, u32[]{:S(2)}) collective-permute-start(f32[3,64,768]{2,1,0:T(8,128)S(1)} %get-tuple-element.50), channel_id=1, source_target_pairs={{0,16},{16,0},{32,48},{48,32},{64,80},{80,64},{96,112},{112,96},{1... | collective-permute-start | bytes 1769480 | tf_op jit(solution)/shard_map/ppermute | solution.py:433
  21.4 10.5 %collective-permute-start.4 = (f32[3,64,640]{2,1,0:T(8,128)S(1)}, f32[3,64,640]{2,1,0:T(8,128)S(1)}, u32[]{:S(2)}, u32[]{:S(2)}) collective-permute-start(f32[3,64,640]{2,1,0:T(8,128)S(1)} %get-tuple-element.51), channel_id=1, source_target_pairs={{0,16},{16,0},{32,48},{48,32},{64,80},{80,64},{96,112},{112,96},{1... | collective-permute-start | bytes 1474568 | tf_op jit(solution)/shard_map/ppermute | solution.py:433
  21.8 13.7 %collective-permute-start.6 = (f32[3,64,128]{2,1,0:T(8,128)S(1)}, f32[3,64,128]{2,1,0:T(8,128)S(1)}, u32[]{:S(2)}, u32[]{:S(2)}) collective-permute-start(f32[3,64,128]{2,1,0:T(8,128)S(1)} %get-tuple-element.55), channel_id=1, source_target_pairs={{0,240},{16,32},{32,16},{48,64},{64,48},{80,96},{96,80},{112,128},... | collective-permute-start | bytes 294920 | tf_op jit(solution)/shard_map/ppermute | solution.py:432
  27.0 4.9 %copy-start.2 = (bf16[2,64,192]{2,1,0:T(8,128)(2,1)S(1)}, bf16[2,64,192]{2,1,0:T(8,128)(2,1)}, u32[]{:S(2)}) copy-start(bf16[2,64,192]{2,1,0:T(8,128)(2,1)} %constant.34.clone.refs_8_.refs_7_) | copy-start | bytes 147460

commit v4 on v3

--- a/solution.py
+++ b/solution.py
@@ -18,13 +18,11 @@
 CW = 256
 MID = ROWS - BLK
 EW = 512
-DW = 512
-AHEAD = 2
 NEAR = (0, 768, 1536, COLS)
 PREP_MIB = 8
 MID_MIB = 6
 EDGE_MIB = 8
-ZONAL_MIB = 16
+ZONAL_MIB = 6
 UNROLL_B = 7
 BF = jnp.bfloat16
 F32 = jnp.float32
@@ -88,7 +86,7 @@
         store(f, r[:ROWS] + r[ROWS:] + dot(g[:ROWS], lo))
 
 
-def prep_kernel(where, u, v, t, m, x1, first, second, rows, wet_rows, cols, wet_cols, sem):
+def prep_kernel(where, u, v, t, m, g, x1, first, second, g_out, rows, wet_rows, cols, wet_cols, sem):
     top = pl.ds(pl.multiple_of(where[0] * (ROWS - HALF), HALF), HALF)
     odd = where[1]
     copies = [pltpu.make_async_copy(m.at[top, :], wet_rows, sem.at[0, 3])]
@@ -100,6 +98,8 @@
                    for i, a in enumerate((u, v, t))]
     for copy in copies:
         copy.start()
+    g_copy = pltpu.make_async_copy(g, g_out, sem.at[3, 0])
+    g_copy.start()
     for copy in copies[:4]:
         copy.wait()
     wet = wet_rows[...].astype(F32)
@@ -118,6 +118,7 @@
                 jnp.where(low, x[:BLK], y[BLK:]),
                 jnp.where(low, y[:BLK], x[BLK:]),
             )
+    g_copy.wait()
 
 
 def corner_kernel(where, first, second, main, wrap, far, near):
@@ -139,31 +140,14 @@
 
 
 def zonal_kernel(core, u, v, t, m, g_ref, zh, zl, zp, *refs):
-    *near, ub, vb, tb, mb, sem = refs
+    near = refs
     g = g_ref[...]
     lower = core[0] == 0
 
-    def copies(j):
-        cols = pl.ds(j * DW, DW)
-        return [
-            pltpu.make_async_copy(src.at[:, cols], dst.at[:, cols], sem.at[i, j])
-            for i, (src, dst) in enumerate(((u, ub), (v, vb), (t, tb), (m, mb)))
-        ]
-
-    for j in range(AHEAD):
-        for copy in copies(j):
-            copy.start()
     for j in range(COLS // CW):
-        if j * CW % DW == 0:
-            k = j * CW // DW
-            for copy in copies(k):
-                copy.wait()
-            if k + AHEAD < COLS // DW:
-                for copy in copies(k + AHEAD):
-                    copy.start()
         cols = pl.ds(j * CW, CW)
-        wet = mb[:, cols].astype(F32)
-        three = (wet * ub[:, cols], wet * vb[:, cols], wet * tb[:, cols])
+        wet = m[:, cols].astype(F32)
+        three = (wet * u[:, cols], wet * v[:, cols], wet * t[:, cols])
         part = max(p for p, start in enumerate(NEAR) if start <= j * CW)
         for i, x in enumerate(three):
             near[part][i, :, pl.ds(j * CW - NEAR[part], CW)] = jnp.where(lower, x[ROWS - HALF:], x[:HALF])
@@ -313,24 +297,24 @@
     return jnp.asarray(np.stack(mats))
 
 
-def prep(core, u, v, t, m):
+def prep(core, u, v, t, m, g):
     side = jax.ShapeDtypeStruct((3, BLK, BLK), F32)
     return pl.pallas_call(
         prep_kernel,
-        out_shape=(jax.ShapeDtypeStruct((3, HALF, COLS), F32), side, side),
-        in_specs=[SMEM] + [HBM] * 4,
-        out_specs=(VMEM,) * 3,
+        out_shape=(jax.ShapeDtypeStruct((3, HALF, COLS), F32), side, side, jax.ShapeDtypeStruct(g.shape, BF)),
+        in_specs=[SMEM] + [HBM] * 5,
+        out_specs=(VMEM,) * 4,
         scratch_shapes=[
             pltpu.VMEM((3, HALF, COLS), F32),
             pltpu.VMEM((HALF, COLS), jnp.int32),
             pltpu.VMEM((2, 3, ROWS, BLK), F32),
             pltpu.VMEM((2, ROWS, BLK), jnp.int32),
-            pltpu.SemaphoreType.DMA((3, 4)),
+            pltpu.SemaphoreType.DMA((4, 4)),
         ],
         compiler_params=params(PREP_MIB),
-        cost_estimate=COST,
+        cost_estimate=pl.CostEstimate(flops=1_000_000, bytes_accessed=60_000_000, transcendentals=0),
         name="prep",
-    )(core, u, v, t, m)
+    )(core, u, v, t, m, g)
 
 
 def corners(where, first, second, main):
@@ -349,28 +333,21 @@
     )(where, first, second, main)
 
 
-def zonal(core, u, v, t, m):
+def zonal(core, u, v, t, m, g):
     half = jax.ShapeDtypeStruct((5 * MID, COLS), BF)
     near = [jax.ShapeDtypeStruct((3, HALF, b - a), F32) for a, b in zip(NEAR[:-1], NEAR[1:])]
     return pl.pallas_call(
         zonal_kernel,
         out_shape=(half, half, jax.ShapeDtypeStruct((5, BLK, COLS), F32), *near),
-        in_specs=[SMEM] + [HBM] * 4 + [VMEM],
+        in_specs=[SMEM] + [VMEM] * 5,
         out_specs=(VMEM,) * (3 + len(near)),
-        scratch_shapes=[
-            pltpu.VMEM((ROWS, COLS), F32),
-            pltpu.VMEM((ROWS, COLS), F32),
-            pltpu.VMEM((ROWS, COLS), F32),
-            pltpu.VMEM((ROWS, COLS), jnp.int32),
-            pltpu.SemaphoreType.DMA((4, COLS // DW)),
-        ],
         compiler_params=params(ZONAL_MIB),
         cost_estimate=COST,
         name="zonal",
-    )(core, u, v, t, m, lon_matrix())
-
-
-def middle(zh, zl, wrap):
+    )(core, u, v, t, m, g)
+
+
+def middle(zh, zl, wrap, g):
     return pl.pallas_call(
         middle_kernel,
         out_shape=(FLUX, FLUX, jax.ShapeDtypeStruct((5, BLK, BLK), F32)),
@@ -386,7 +363,7 @@
         compiler_params=params(MID_MIB),
         cost_estimate=COST,
         name="middle",
-    )(zh, zl, wrap, lon_matrix(), lat_matrix())
+    )(zh, zl, wrap, g, lat_matrix())
 
 
 def edge(sel, east, north, zp, zpw, pieces, name):
@@ -419,19 +396,19 @@
     odd_pairs = [(i, i - 1 + 2 * (i % 2)) for i in range(1, nlat - 1)]
 
     sel = core.astype(jnp.int32).reshape(1)
-    u, v, t, m = (pltpu.with_memory_space_constraint(a, pltpu.HBM) for a in (u, v, t, m))
+    held = [pltpu.with_memory_space_constraint(a, pltpu.HBM) for a in (u, v, t, m, lon_matrix())]
     where = jnp.stack([core, odd]).astype(jnp.int32)
-    x1, first, second = prep(where, u, v, t, m)
+    x1, first, second, g = prep(where, *held)
     x1 = lax.ppermute(x1, "lon", across)
     first = lax.ppermute(first, "lat", even_pairs)
     second = lax.ppermute(second, "lat", odd_pairs)
-    zh, zl, zp, *near = zonal(sel, u, v, t, m)
+    zh, zl, zp, *near = zonal(sel, u, v, t, m, g)
     zh, zl, first, second = lax.optimization_barrier((zh, zl, first, second))
     wrap, x2, near[-1] = corners(where, first, second, near[-1])
     x2, near, zh, zl = lax.optimization_barrier((x2, near, zh, zl))
     x2 = lax.ppermute(x2, "lon", across)
     near = [lax.ppermute(part, "lon", inside) for part in near]
-    east, north, zpw = middle(zh, zl, wrap)
+    east, north, zpw = middle(zh, zl, wrap, g)
     east, north = edge(1 - sel, east, north, zp, zpw, near, "edge_near")
     return edge(sel, east, north, zp, zpw, (x1, x2), "edge_far")
 

time: 39.5 us -> 37.5 us (0.949)
  Pallas kernels: 22.4 us -> 20.6 us
    pallas_call x1, Pallas kernels: 6.93 us -> 4.76 us  [zonal(): pl.pallas_call(zonal_kernel, out_shape=(half, half, jax.ShapeDtypeStruct(...]
  transfers between devices with their start and end apart: 7 -> 7, of which waited for: 0 -> 0; matrix products, arithmetic and copies ran while one was open for 0% -> 0% of each run, Pallas kernels for 41% -> 37%
where the time goes in v4:
time: 37.5 us; the launch traced here: 37.4 us
  Pallas kernels  20.6 us (55%)
  starting transfers between devices  15.8 us (42%)
  between operations  0.97 us (3%)
    pallas_call x2, Pallas kernels, edge(): pl.pallas_call(functools.partial(edge_kernel, len(pieces)), out_shape=(FL...  7.27 us
    ppermute x1, starting transfers between devices, shards(): second = lax.ppermute(second, 'lat', odd_pairs)  5.93 us
    ppermute x1, starting transfers between devices, shards(): x2 = lax.ppermute(x2, 'lon', across)  5.08 us
    pallas_call x1, Pallas kernels, middle(): pl.pallas_call(middle_kernel, out_shape=(FLUX, FLUX, jax.ShapeDtypeStruct...  4.84 us
    pallas_call x1, Pallas kernels, zonal(): pl.pallas_call(zonal_kernel, out_shape=(half, half, jax.ShapeDtypeStruct(...  4.76 us
    pallas_call x1, Pallas kernels, prep(): pl.pallas_call(prep_kernel, out_shape=(jax.ShapeDtypeStruct((3, HALF, COL...  2.98 us
    ppermute x3, starting transfers between devices, shards(): near = [lax.ppermute(part, 'lon', inside) for part in near]  1.7 us
    ppermute x1, starting transfers between devices, shards(): first = lax.ppermute(first, 'lat', even_pairs)  1.64 us
  transfers between devices with their start and end apart: 7, of which 0 were waited for; matrix products, arithmetic and copies ran while one was open for 0% of the time, Pallas kernels for 37%

profile of v4, /device:TPU:31, one launch (start us, length us, event | category | flops | bytes accessed | tf_op | source)
XLA Modules:
  0.0 37.4 jit_solution(4475684876656969372)
XLA Ops:
  0.6 0.1 pad_add_fusion.where
  0.7 3.0 %prep.1 = (f32[3,64,2048]{2,1,0:T(8,128)S(1)}, f32[3,128,128]{2,1,0:T(8,128)S(1)}, f32[3,128,128]{2,1,0:T(8,128)S(1)}, bf16[512,256]{1,0:T(8,128)(2,1)S(1)}) custom-call(s32[2]{0:T(128)S(1)} %pad_add_fusion.where, f32[256,2048]{1,0:T(8,128)} %u.3, f32[256,2048]{1,0:T(8,128)} %v.3, f32[256,2048]{1,0:T(8,128)} %t.3, s32[256,2048]{1,0:T(8,128)} %m.3, ...), custom_call_target="tpu_custom_call" | custom-call | flops 1000000 | bytes 60000000 | tf_op jit(solution)/shard_map/prep/pallas_call | solution.py:302
  3.7 1.4 %collective-permute-start.5 = (f32[3,64,2048]{2,1,0:T(8,128)S(1)}, f32[3,64,2048]{2,1,0:T(8,128)S(1)}, u32[]{:S(2)}, u32[]{:S(2)}) collective-permute-start(f32[3,64,2048]{2,1,0:T(8,128)S(1)} %get-tuple-element.56), channel_id=1, source_target_pairs={{0,240},{16,32},{32,16},{48,64},{64,48},{80,96},{96,80},{112,128},... | collective-permute-start | bytes 4718600 | tf_op jit(solution)/shard_map/ppermute | solution.py:402
  5.2 1.6 %collective-permute-start = (f32[3,128,128]{2,1,0:T(8,128)S(1)}, f32[3,128,128]{2,1,0:T(8,128)S(1)}, u32[]{:S(2)}, u32[]{:S(2)}) collective-permute-start(f32[3,128,128]{2,1,0:T(8,128)S(1)} %get-tuple-element.33), channel_id=1, source_target_pairs={{0,1},{1,0},{2,3},{3,2},{4,5},{5,4},{6,7},{7,6},{8,9},{9,8},{10,11... | collective-permute-start | bytes 589832 | tf_op jit(solution)/shard_map/ppermute | solution.py:403
  6.8 5.9 %collective-permute-start.1 = (f32[3,128,128]{2,1,0:T(8,128)S(1)}, f32[3,128,128]{2,1,0:T(8,128)S(1)}, u32[]{:S(2)}, u32[]{:S(2)}) collective-permute-start(f32[3,128,128]{2,1,0:T(8,128)S(1)} %get-tuple-element.34), channel_id=1, source_target_pairs={{1,2},{2,1},{3,4},{4,3},{5,6},{6,5},{7,8},{8,7},{9,10},{10,9},{11,... | collective-permute-start | bytes 589832 | tf_op jit(solution)/shard_map/ppermute | solution.py:404
  12.7 0.0 copy-done
  12.7 0.0 copy-done.1
  12.8 0.0 copy-start.4
  12.8 4.8 %zonal.1 = (bf16[640,2048]{1,0:T(8,128)(2,1)S(1)}, bf16[640,2048]{1,0:T(8,128)(2,1)S(1)}, f32[5,128,2048]{2,1,0:T(8,128)S(1)}, f32[3,64,768]{2,1,0:T(8,128)S(1)}...) custom-call(s32[1]{0:T(128)} %bitcast.core.refs_0_, f32[256,2048]{1,0:T(8,128)S(1)} %copy-done, ...), custom_call_target="tpu_custom_call" | custom-call | flops 1000000 | bytes 1000000 | tf_op jit(solution)/shard_map/zonal/pallas_call | solution.py:339
  17.5 0.0 collective-permute-done.first
  17.6 0.0 collective-permute-done.1.second
  17.6 0.7 %corners.1 = (f32[3,256,128]{2,1,0:T(8,128)S(1)}, f32[3,64,128]{2,1,0:T(8,128)S(1)}, f32[3,64,640]{2,1,0:T(8,128)S(1)}) custom-call(s32[2]{0:T(128)S(1)} %pad_add_fusion.where, f32[3,128,128]{2,1,0:T(8,128)S(1)} %collective-permute-done.first, f32[3,128,128]{2,1,0:T(8,128)S(1)} %collective-permute-done.1.second, f32[3,64,512]{2,1,0:T(8,128)S(1)} %get-tuple-element.37.main), custom_call_target="tpu_custom_call" | custom-call | flops 1000000 | bytes 1000000 | tf_op jit(solution)/shard_map/corners/pallas_call | solution.py:321
  18.3 1.2 %collective-permute-start.2 = (f32[3,64,768]{2,1,0:T(8,128)S(1)}, f32[3,64,768]{2,1,0:T(8,128)S(1)}, u32[]{:S(2)}, u32[]{:S(2)}) collective-permute-start(f32[3,64,768]{2,1,0:T(8,128)S(1)} %get-tuple-element.51), channel_id=1, source_target_pairs={{0,16},{16,0},{32,48},{48,32},{64,80},{80,64},{96,112},{112,96},{1... | collective-permute-start | bytes 1769480 | tf_op jit(solution)/shard_map/ppermute | solution.py:410
  19.5 0.1 collective-permute-start.3
  19.6 0.4 %collective-permute-start.4 = (f32[3,64,640]{2,1,0:T(8,128)S(1)}, f32[3,64,640]{2,1,0:T(8,128)S(1)}, u32[]{:S(2)}, u32[]{:S(2)}) collective-permute-start(f32[3,64,640]{2,1,0:T(8,128)S(1)} %get-tuple-element.53), channel_id=1, source_target_pairs={{0,16},{16,0},{32,48},{48,32},{64,80},{80,64},{96,112},{112,96},{1... | collective-permute-start | bytes 1474568 | tf_op jit(solution)/shard_map/ppermute | solution.py:410
  20.0 5.1 %collective-permute-start.6 = (f32[3,64,128]{2,1,0:T(8,128)S(1)}, f32[3,64,128]{2,1,0:T(8,128)S(1)}, u32[]{:S(2)}, u32[]{:S(2)}) collective-permute-start(f32[3,64,128]{2,1,0:T(8,128)S(1)} %get-tuple-element.57), channel_id=1, source_target_pairs={{0,240},{16,32},{32,16},{48,64},{64,48},{80,96},{96,80},{112,128},... | collective-permute-start | bytes 294920 | tf_op jit(solution)/shard_map/ppermute | solution.py:409
  25.1 4.8 %middle.1 = (f32[256,2048]{1,0:T(8,128)}, f32[256,2048]{1,0:T(8,128)}, f32[5,128,128]{2,1,0:T(8,128)S(1)}) custom-call(bf16[640,2048]{1,0:T(8,128)(2,1)S(1)} %get-tuple-element.44.zh, bf16[640,2048]{1,0:T(8,128)(2,1)S(1)} %get-tuple-element.45.zl, f32[3,256,128]{2,1,0:T(8,128)S(1)} %get-tuple-element.46.wrap, bf16[512,256]{1,0:T(8,128)(2,1)S(1)} %get-tuple-element.30.g_ref, ...), custom_call_target="tpu_custom_call" | custom-call | flops 1000000 | bytes 1000000 | tf_op jit(solution)/shard_map/middle/pallas_call | solution.py:351
  29.9 0.0 collective-permute-done.4.refs_7_
  29.9 0.0 collective-permute-done.2.refs_5_
  29.9 0.0 collective-permute-done.3.refs_6_
  30.0 3.6 %edge_near.1 = (f32[256,2048]{1,0:T(8,128)}, f32[256,2048]{1,0:T(8,128)}) custom-call(s32[1]{0:T(128)S(6)} %sub.3.refs_0_, f32[256,2048]{1,0:T(8,128)} %get-tuple-element.47.refs_1_, f32[256,2048]{1,0:T(8,128)} %get-tuple-element.48.refs_2_, f32[5,128,2048]{2,1,0:T(8,128)S(1)} %get-tuple-element.49.refs_3_, ...), custom_call_target="tpu_custom_call", output_to_operand_aliasing={{0}: (1, {}), {1}: (2, {})} | custom-call | flops 1000000 | bytes 1000000 | tf_op jit(solution)/shard_map/edge_near/pallas_call | solution.py:370
  33.6 0.0 collective-permute-done.6.refs_6_
  33.6 0.0 collective-permute-done.5.refs_5_
  33.6 3.6 %edge_far.1 = (f32[256,2048]{1,0:T(8,128)}, f32[256,2048]{1,0:T(8,128)}) custom-call(s32[1]{0:T(128)} %bitcast.core.refs_0_, f32[256,2048]{1,0:T(8,128)} %get-tuple-element.54.refs_1_, f32[256,2048]{1,0:T(8,128)} %get-tuple-element.55.refs_2_, f32[5,128,2048]{2,1,0:T(8,128)S(1)} %get-tuple-element.49.refs_3_, ...), custom_call_target="tpu_custom_call", output_to_operand_aliasing={{0}: (1, {}), {1}: (2, {})} | custom-call | flops 1000000 | bytes 1000000 | tf_op jit(solution)/shard_map/edge_far/pallas_call | solution.py:370
  (9 shorter events, 0.0 us)
Async XLA Ops:
  0.7 12.0 %copy-start = (f32[256,2048]{1,0:T(8,128)S(1)}, f32[256,2048]{1,0:T(8,128)}, u32[]{:S(2)}) copy-start(f32[256,2048]{1,0:T(8,128)} %u.3) | copy-start | bytes 6291460
  0.7 12.0 %copy-start.1 = (f32[256,2048]{1,0:T(8,128)S(1)}, f32[256,2048]{1,0:T(8,128)}, u32[]{:S(2)}) copy-start(f32[256,2048]{1,0:T(8,128)} %v.3) | copy-start | bytes 6291460
  0.7 12.0 %copy-start.2 = (f32[256,2048]{1,0:T(8,128)S(1)}, f32[256,2048]{1,0:T(8,128)}, u32[]{:S(2)}) copy-start(f32[256,2048]{1,0:T(8,128)} %t.3) | copy-start | bytes 6291460
  0.7 12.0 %copy-start.3 = (s32[256,2048]{1,0:T(8,128)S(1)}, s32[256,2048]{1,0:T(8,128)}, u32[]{:S(2)}) copy-start(s32[256,2048]{1,0:T(8,128)} %m.3) | copy-start | bytes 6291460
  3.7 29.9 %collective-permute-start.5 = (f32[3,64,2048]{2,1,0:T(8,128)S(1)}, f32[3,64,2048]{2,1,0:T(8,128)S(1)}, u32[]{:S(2)}, u32[]{:S(2)}) collective-permute-start(f32[3,64,2048]{2,1,0:T(8,128)S(1)} %get-tuple-element.56), channel_id=1, source_target_pairs={{0,240},{16,32},{32,16},{48,64},{64,48},{80,96},{96,80},{112,128},... | collective-permute-start | bytes 4718600 | tf_op jit(solution)/shard_map/ppermute | solution.py:402
  5.2 12.4 %collective-permute-start = (f32[3,128,128]{2,1,0:T(8,128)S(1)}, f32[3,128,128]{2,1,0:T(8,128)S(1)}, u32[]{:S(2)}, u32[]{:S(2)}) collective-permute-start(f32[3,128,128]{2,1,0:T(8,128)S(1)} %get-tuple-element.33), channel_id=1, source_target_pairs={{0,1},{1,0},{2,3},{3,2},{4,5},{5,4},{6,7},{7,6},{8,9},{9,8},{10,11... | collective-permute-start | bytes 589832 | tf_op jit(solution)/shard_map/ppermute | solution.py:403
  6.8 10.8 %collective-permute-start.1 = (f32[3,128,128]{2,1,0:T(8,128)S(1)}, f32[3,128,128]{2,1,0:T(8,128)S(1)}, u32[]{:S(2)}, u32[]{:S(2)}) collective-permute-start(f32[3,128,128]{2,1,0:T(8,128)S(1)} %get-tuple-element.34), channel_id=1, source_target_pairs={{1,2},{2,1},{3,4},{4,3},{5,6},{6,5},{7,8},{8,7},{9,10},{10,9},{11,... | collective-permute-start | bytes 589832 | tf_op jit(solution)/shard_map/ppermute | solution.py:404
  12.8 12.3 %copy-start.4 = (bf16[256,256]{1,0:T(8,128)(2,1)S(1)}, bf16[256,256]{1,0:T(8,128)(2,1)}, u32[]{:S(2)}) copy-start(bf16[256,256]{1,0:T(8,128)(2,1)} %constant.33.clone.w_ref.refs_9_.refs_8_) | copy-start | bytes 393220
  18.3 11.6 %collective-permute-start.2 = (f32[3,64,768]{2,1,0:T(8,128)S(1)}, f32[3,64,768]{2,1,0:T(8,128)S(1)}, u32[]{:S(2)}, u32[]{:S(2)}) collective-permute-start(f32[3,64,768]{2,1,0:T(8,128)S(1)} %get-tuple-element.51), channel_id=1, source_target_pairs={{0,16},{16,0},{32,48},{48,32},{64,80},{80,64},{96,112},{112,96},{1... | collective-permute-start | bytes 1769480 | tf_op jit(solution)/shard_map/ppermute | solution.py:410
  19.5 10.5 %collective-permute-start.3 = (f32[3,64,768]{2,1,0:T(8,128)S(1)}, f32[3,64,768]{2,1,0:T(8,128)S(1)}, u32[]{:S(2)}, u32[]{:S(2)}) collective-permute-start(f32[3,64,768]{2,1,0:T(8,128)S(1)} %get-tuple-element.52), channel_id=1, source_target_pairs={{0,16},{16,0},{32,48},{48,32},{64,80},{80,64},{96,112},{112,96},{1... | collective-permute-start | bytes 1769480 | tf_op jit(solution)/shard_map/ppermute | solution.py:410
  19.6 10.3 %collective-permute-start.4 = (f32[3,64,640]{2,1,0:T(8,128)S(1)}, f32[3,64,640]{2,1,0:T(8,128)S(1)}, u32[]{:S(2)}, u32[]{:S(2)}) collective-permute-start(f32[3,64,640]{2,1,0:T(8,128)S(1)} %get-tuple-element.53), channel_id=1, source_target_pairs={{0,16},{16,0},{32,48},{48,32},{64,80},{80,64},{96,112},{112,96},{1... | collective-permute-start | bytes 1474568 | tf_op jit(solution)/shard_map/ppermute | solution.py:410
  20.0 13.6 %collective-permute-start.6 = (f32[3,64,128]{2,1,0:T(8,128)S(1)}, f32[3,64,128]{2,1,0:T(8,128)S(1)}, u32[]{:S(2)}, u32[]{:S(2)}) collective-permute-start(f32[3,64,128]{2,1,0:T(8,128)S(1)} %get-tuple-element.57), channel_id=1, source_target_pairs={{0,240},{16,32},{32,16},{48,64},{64,48},{80,96},{96,80},{112,128},... | collective-permute-start | bytes 294920 | tf_op jit(solution)/shard_map/ppermute | solution.py:409
  25.1 4.9 %copy-start.5 = (bf16[2,64,192]{2,1,0:T(8,128)(2,1)S(1)}, bf16[2,64,192]{2,1,0:T(8,128)(2,1)}, u32[]{:S(2)}) copy-start(bf16[2,64,192]{2,1,0:T(8,128)(2,1)} %constant.34.clone.refs_8_.refs_7_) | copy-start | bytes 147460
